TPU v7x, 32 devices: a whole 2x2x4 slice. The times are simulated.
32 devices in a mesh: section: 2 (over y), expert: 16 (over z, x, core).
Axes of the slice: x: 2, y: 2, z: 4, core: 2. Of those that a mesh axis runs over, the one named last changes fastest.
Arguments:
- acts: bfloat16 [2, 4, 512, 1024], P('section', None, 'expert'), may hold values from -6 to 6
- carried: bfloat16 [2, 512, 1024], P('section', 'expert'), may hold values from -6 to 6
- loss_grad: bfloat16 [4, 512, 1024], P(None, 'expert'), may hold values from -6 to 6
- expert_ids: int32 [2, 4, 512, 8], P('section', None, 'expert'), may hold values from 0 to 15, all different within a row; in each aligned block of 32 rows (0 to 31, 32 to 63, ..., all dimensions but the last counted through in order) at most 24 rows name the same one
- probs: float32 [2, 4, 512, 8], P('section', None, 'expert'), may hold values from 0.1 to 0.4
- w_gate: bfloat16 [2, 16, 1024, 384], P('section', 'expert'), may hold values from -0.1875 to 0.1875
- w_up: bfloat16 [2, 16, 1024, 384], P('section', 'expert'), may hold values from -0.1875 to 0.1875
- w_down: bfloat16 [2, 16, 384, 1024], P('section', 'expert'), may hold values from -0.3125 to 0.3125
Outputs:
- out_grad: bfloat16 [2, 4, 512, 1024], P('section', None, 'expert')
- down_grad: bfloat16 [2, 16, 384, 1024], P('section', 'expert')
Inputs may be any that keep to these rules, and one draw needn't show every extreme that they name: `expert_ids`: in each aligned block of 32 tokens of one section and tick, no expert is named by more than 24 of the block's pairs, and in every draw some block has an expert named by exactly 24.
All inputs are finite; a program needn't handle non-finite values.
Results may differ from a plain program's by a relative error of at most 0.0095.
Values may be sent and summed in bfloat16 or wider, within the bound.
A program may use at most 64 MiB of HBM per device.

v0:
```python
import jax
import jax.numpy as jnp
from jax import lax
from jax.sharding import PartitionSpec as P

TOPK = 8


def passed_along(value, axis, steps):
    count = lax.axis_size(axis)
    leading, last = (max(0, -steps), min(count, count - steps))
    return lax.ppermute(value, axis, [(source, source + steps) for source in range(leading, last)])


def slot_tables(expert_ids, probs, experts, slot_rows):
    tokens_here, choices_here = expert_ids.shape
    onehot = (expert_ids[:, :, None] == jnp.arange(experts, dtype=jnp.int32)[None, None, :]).astype(
        jnp.int32
    )
    pairs = onehot.reshape(tokens_here * choices_here, experts)
    before = jnp.cumsum(pairs, axis=0) - pairs
    position = jnp.sum(before * pairs, axis=1).reshape(tokens_here, choices_here)
    target = expert_ids * slot_rows + position
    match = target[None, :, :] == jnp.arange(experts * slot_rows, dtype=jnp.int32)[:, None, None]
    select = jnp.any(match, axis=2).astype(jnp.bfloat16)
    weight = jnp.sum(jnp.where(match, probs[None, :, :], 0.0), axis=(1, 2))
    return (select, weight)


def select_rows(select, source):
    return jnp.dot(select, source, preferred_element_type=jnp.float32)


def forward_parts(input_rows, gate_weight, up_weight):
    gate_pre = jnp.dot(input_rows, gate_weight, preferred_element_type=jnp.float32)
    up_pre = jnp.dot(input_rows, up_weight, preferred_element_type=jnp.float32)
    return (gate_pre, up_pre)


def expert_backward(gate_pre, up_pre, grad_rows, gate_weight, up_weight, down_weight):
    contract = (((1,), (1,)), ((), ()))
    sigma = jax.nn.sigmoid(gate_pre)
    active = gate_pre * sigma
    hidden = (active * up_pre).astype(jnp.bfloat16)
    hidden_grad = lax.dot_general(
        grad_rows, down_weight, contract, preferred_element_type=jnp.float32
    )
    gate_grad = (hidden_grad * up_pre * sigma * (1.0 + gate_pre * (1.0 - sigma))).astype(
        jnp.bfloat16
    )
    up_grad = (hidden_grad * active).astype(jnp.bfloat16)
    row_grad = lax.dot_general(gate_grad, gate_weight, contract, preferred_element_type=jnp.float32)
    row_grad = row_grad + lax.dot_general(
        up_grad, up_weight, contract, preferred_element_type=jnp.float32
    )
    return (row_grad.astype(jnp.bfloat16), hidden)


def per_device(acts, carried, loss_grad, expert_ids, probs, w_gate, w_up, w_down):
    experts = lax.axis_size("expert")
    ticks_here = acts.shape[1]
    tokens_here = acts.shape[2]
    width = acts.shape[3]
    slot_rows = min(tokens_here, 3 * tokens_here * TOPK // (2 * experts))
    gate_weight = w_gate[0, 0]
    up_weight = w_up[0, 0]
    down_weight = w_down[0, 0]
    is_last = lax.axis_index("section") == lax.axis_size("section") - 1
    tables = [
        slot_tables(expert_ids[0, moment], probs[0, moment], experts, slot_rows)
        for moment in range(ticks_here)
    ]
    rows_contract = (((0,), (0,)), ((), ()))
    incoming = jnp.where(is_last, loss_grad[0], carried[0])
    results = []
    down_sum = jnp.zeros((down_weight.shape[0], width), jnp.float32)
    for moment in range(ticks_here):
        select, weight = tables[moment]
        grad_rows = (
            (select_rows(select, incoming) * weight[:, None])
            .astype(jnp.bfloat16)
            .reshape(experts, slot_rows, width)
        )
        input_rows = (
            select_rows(select, acts[0, moment])
            .astype(jnp.bfloat16)
            .reshape(experts, slot_rows, width)
        )
        received_input, received_grad = (
            lax.all_to_all(input_rows, "expert", split_axis=0, concat_axis=0, tiled=True),
            lax.all_to_all(grad_rows, "expert", split_axis=0, concat_axis=0, tiled=True),
        )
        gate_pre, up_pre = forward_parts(received_input.reshape(-1, width), gate_weight, up_weight)
        flat_grad = received_grad.reshape(-1, width)
        row_grad, hidden = expert_backward(
            gate_pre, up_pre, flat_grad, gate_weight, up_weight, down_weight
        )
        returned = lax.all_to_all(
            row_grad.reshape(experts, slot_rows, width),
            "expert",
            split_axis=0,
            concat_axis=0,
            tiled=True,
        )
        gathered = lax.dot_general(
            select, returned.reshape(-1, width), rows_contract, preferred_element_type=jnp.float32
        )
        result = (incoming.astype(jnp.float32) + gathered).astype(jnp.bfloat16)
        results.append(result)
        down_sum = down_sum + lax.dot_general(
            hidden, flat_grad, rows_contract, preferred_element_type=jnp.float32
        )
        if moment + 1 < ticks_here:
            arriving = passed_along(result, "section", -1)
            incoming = jnp.where(is_last, loss_grad[moment + 1], arriving)
    out_grad = jnp.stack(results, axis=0)[None]
    return (out_grad, down_sum.astype(jnp.bfloat16)[None, None])


def solution(mesh):
    return jax.shard_map(
        per_device,
        mesh=mesh,
        in_specs=(
            P("section", None, "expert", None),
            P("section", "expert", None),
            P(None, "expert", None),
            P("section", None, "expert", None),
            P("section", None, "expert", None),
            P("section", "expert", None, None),
            P("section", "expert", None, None),
            P("section", "expert", None, None),
        ),
        out_specs=(P("section", None, "expert", None), P("section", "expert", None, None)),
        check_vma=False,
    )
```

profile of v0, /device:TPU:0, one launch (start us, length us, event | category | flops | bytes accessed | tf_op | source)
XLA Modules:
  0.0 319.2 jit_solution(14465334493668054591)
XLA Ops:
  0.7 1.4 fusion.99
  3.6 2.1 convolution_convert_fusion.3
  5.7 7.4 %all-to-all-start.1 = ((bf16[16,24,1024]{2,1,0:T(8,128)(2,1)}), bf16[16,24,1024]{2,1,0:T(8,128)(2,1)S(1)}, u32[]{:S(2)}, u32[]{:S(2)}) async-start(bf16[16,24,1024]{2,1,0:T(8,128)(2,1)} %bitcast.8), calls=%async_computation.1 | async-start | bytes 1572864 | tf_op jit(solution)/shard_map/all_to_all | solution.py:90
  13.9 1.3 multiply_convert_fusion.3
  15.3 16.5 %all-to-all-done.1 = bf16[16,24,1024]{2,1,0:T(8,128)(2,1)S(1)} async-done(((bf16[16,24,1024]{2,1,0:T(8,128)(2,1)}), bf16[16,24,1024]{2,1,0:T(8,128)(2,1)S(1)}, u32[]{:S(2)}, u32[]{:S(2)}) %all-to-all-start.1) | async-done | bytes 786464 | tf_op jit(solution)/shard_map/all_to_all | solution.py:90
  31.8 5.7 %all-to-all-start = ((bf16[16,24,1024]{2,1,0:T(8,128)(2,1)}), bf16[16,24,1024]{2,1,0:T(8,128)(2,1)}, u32[]{:S(2)}, u32[]{:S(2)}) async-start(bf16[16,24,1024]{2,1,0:T(8,128)(2,1)} %bitcast.4), calls=%async_computation | async-start | bytes 1572864 | tf_op jit(solution)/shard_map/all_to_all | solution.py:91
  37.5 1.4 fusion.16
  38.9 1.4 fusion.28
  40.3 16.0 %all-to-all-done = bf16[16,24,1024]{2,1,0:T(8,128)(2,1)} async-done(((bf16[16,24,1024]{2,1,0:T(8,128)(2,1)}), bf16[16,24,1024]{2,1,0:T(8,128)(2,1)}, u32[]{:S(2)}, u32[]{:S(2)}) %all-to-all-start) | async-done | bytes 786464 | tf_op jit(solution)/shard_map/all_to_all | solution.py:91
  56.2 1.8 fusion.36
  58.7 1.5 add_convert_fusion.4
  60.2 5.5 %all-to-all-start.2 = ((bf16[16,24,1024]{2,1,0:T(8,128)(2,1)}), bf16[16,24,1024]{2,1,0:T(8,128)(2,1)S(1)}, u32[]{:S(2)}, u32[]{:S(2)}) async-start(bf16[16,24,1024]{2,1,0:T(8,128)(2,1)} %bitcast.266), calls=%async_computation.2 | async-start | bytes 1572864 | tf_op jit(solution)/shard_map/all_to_all | solution.py:98
  67.2 2.2 convolution_convert_fusion.2
  69.4 15.1 %all-to-all-done.2 = bf16[16,24,1024]{2,1,0:T(8,128)(2,1)S(1)} async-done(((bf16[16,24,1024]{2,1,0:T(8,128)(2,1)}), bf16[16,24,1024]{2,1,0:T(8,128)(2,1)S(1)}, u32[]{:S(2)}, u32[]{:S(2)}) %all-to-all-start.2) | async-done | bytes 786464 | tf_op jit(solution)/shard_map/all_to_all | solution.py:98
  84.4 0.9 copy-done.5
  85.3 5.5 %all-to-all-start.4 = ((bf16[16,24,1024]{2,1,0:T(8,128)(2,1)}), bf16[16,24,1024]{2,1,0:T(8,128)(2,1)S(1)}, u32[]{:S(2)}, u32[]{:S(2)}) async-start(bf16[16,24,1024]{2,1,0:T(8,128)(2,1)} %bitcast.261), calls=%async_computation.4 | async-start | bytes 1572864 | tf_op jit(solution)/shard_map/all_to_all | solution.py:90
  91.6 1.4 fusion.1
  92.9 1.3 collective-permute-start
  94.4 4.9 %collective-permute-done = bf16[32,1024]{1,0:T(8,128)(2,1)S(1)} collective-permute-done((bf16[32,1024]{1,0:T(8,128)(2,1)S(1)}, bf16[32,1024]{1,0:T(8,128)(2,1)S(1)}, u32[]{:S(2)}, u32[]{:S(2)}) %collective-permute-start) | collective-permute-done | bytes 65568 | tf_op jit(solution)/shard_map/ppermute | solution.py:12
  99.3 1.3 multiply_convert_fusion.2
  100.6 8.9 %all-to-all-done.4 = bf16[16,24,1024]{2,1,0:T(8,128)(2,1)S(1)} async-done(((bf16[16,24,1024]{2,1,0:T(8,128)(2,1)}), bf16[16,24,1024]{2,1,0:T(8,128)(2,1)S(1)}, u32[]{:S(2)}, u32[]{:S(2)}) %all-to-all-start.4) | async-done | bytes 786464 | tf_op jit(solution)/shard_map/all_to_all | solution.py:90
  109.5 5.5 %all-to-all-start.3 = ((bf16[16,24,1024]{2,1,0:T(8,128)(2,1)}), bf16[16,24,1024]{2,1,0:T(8,128)(2,1)}, u32[]{:S(2)}, u32[]{:S(2)}) async-start(bf16[16,24,1024]{2,1,0:T(8,128)(2,1)} %bitcast.262), calls=%async_computation.3 | async-start | bytes 1572864 | tf_op jit(solution)/shard_map/all_to_all | solution.py:91
  115.0 1.4 fusion.12
  116.4 1.4 fusion.25
  117.8 16.0 %all-to-all-done.3 = bf16[16,24,1024]{2,1,0:T(8,128)(2,1)} async-done(((bf16[16,24,1024]{2,1,0:T(8,128)(2,1)}), bf16[16,24,1024]{2,1,0:T(8,128)(2,1)}, u32[]{:S(2)}, u32[]{:S(2)}) %all-to-all-start.3) | async-done | bytes 786464 | tf_op jit(solution)/shard_map/all_to_all | solution.py:91
  133.8 1.8 fusion.34
  136.3 1.5 add_convert_fusion.3
  137.8 5.6 %all-to-all-start.5 = ((bf16[16,24,1024]{2,1,0:T(8,128)(2,1)}), bf16[16,24,1024]{2,1,0:T(8,128)(2,1)S(1)}, u32[]{:S(2)}, u32[]{:S(2)}) async-start(bf16[16,24,1024]{2,1,0:T(8,128)(2,1)} %bitcast.267), calls=%async_computation.5 | async-start | bytes 1572864 | tf_op jit(solution)/shard_map/all_to_all | solution.py:98
  144.9 2.2 convolution_convert_fusion.1
  147.1 15.1 %all-to-all-done.5 = bf16[16,24,1024]{2,1,0:T(8,128)(2,1)S(1)} async-done(((bf16[16,24,1024]{2,1,0:T(8,128)(2,1)}), bf16[16,24,1024]{2,1,0:T(8,128)(2,1)S(1)}, u32[]{:S(2)}, u32[]{:S(2)}) %all-to-all-start.5) | async-done | bytes 786464 | tf_op jit(solution)/shard_map/all_to_all | solution.py:98
  163.0 5.5 %all-to-all-start.7 = ((bf16[16,24,1024]{2,1,0:T(8,128)(2,1)}), bf16[16,24,1024]{2,1,0:T(8,128)(2,1)S(1)}, u32[]{:S(2)}, u32[]{:S(2)}) async-start(bf16[16,24,1024]{2,1,0:T(8,128)(2,1)} %bitcast.260), calls=%async_computation.7 | async-start | bytes 1572864 | tf_op jit(solution)/shard_map/all_to_all | solution.py:90
  169.3 1.4 add_convert_fusion.7
  170.6 1.3 collective-permute-start.1
  172.1 4.9 %collective-permute-done.1 = bf16[32,1024]{1,0:T(8,128)(2,1)S(1)} collective-permute-done((bf16[32,1024]{1,0:T(8,128)(2,1)S(1)}, bf16[32,1024]{1,0:T(8,128)(2,1)S(1)}, u32[]{:S(2)}, u32[]{:S(2)}) %collective-permute-start.1) | collective-permute-done | bytes 65568 | tf_op jit(solution)/shard_map/ppermute | solution.py:12
  177.0 1.3 multiply_convert_fusion.1
  178.3 8.9 %all-to-all-done.7 = bf16[16,24,1024]{2,1,0:T(8,128)(2,1)S(1)} async-done(((bf16[16,24,1024]{2,1,0:T(8,128)(2,1)}), bf16[16,24,1024]{2,1,0:T(8,128)(2,1)S(1)}, u32[]{:S(2)}, u32[]{:S(2)}) %all-to-all-start.7) | async-done | bytes 786464 | tf_op jit(solution)/shard_map/all_to_all | solution.py:90
  187.2 5.5 %all-to-all-start.6 = ((bf16[16,24,1024]{2,1,0:T(8,128)(2,1)}), bf16[16,24,1024]{2,1,0:T(8,128)(2,1)}, u32[]{:S(2)}, u32[]{:S(2)}) async-start(bf16[16,24,1024]{2,1,0:T(8,128)(2,1)} %bitcast.263), calls=%async_computation.6 | async-start | bytes 1572864 | tf_op jit(solution)/shard_map/all_to_all | solution.py:91
  192.8 1.4 fusion.8
  194.2 1.4 fusion.22
  195.6 15.9 %all-to-all-done.6 = bf16[16,24,1024]{2,1,0:T(8,128)(2,1)} async-done(((bf16[16,24,1024]{2,1,0:T(8,128)(2,1)}), bf16[16,24,1024]{2,1,0:T(8,128)(2,1)}, u32[]{:S(2)}, u32[]{:S(2)}) %all-to-all-start.6) | async-done | bytes 786464 | tf_op jit(solution)/shard_map/all_to_all | solution.py:91
  211.5 1.8 fusion.32
  214.0 1.5 add_convert_fusion.2
  215.5 5.5 %all-to-all-start.8 = ((bf16[16,24,1024]{2,1,0:T(8,128)(2,1)}), bf16[16,24,1024]{2,1,0:T(8,128)(2,1)S(1)}, u32[]{:S(2)}, u32[]{:S(2)}) async-start(bf16[16,24,1024]{2,1,0:T(8,128)(2,1)} %bitcast.265), calls=%async_computation.8 | async-start | bytes 1572864 | tf_op jit(solution)/shard_map/all_to_all | solution.py:98
  222.5 2.2 convolution_convert_fusion
  224.7 15.1 %all-to-all-done.8 = bf16[16,24,1024]{2,1,0:T(8,128)(2,1)S(1)} async-done(((bf16[16,24,1024]{2,1,0:T(8,128)(2,1)}), bf16[16,24,1024]{2,1,0:T(8,128)(2,1)S(1)}, u32[]{:S(2)}, u32[]{:S(2)}) %all-to-all-start.8) | async-done | bytes 786464 | tf_op jit(solution)/shard_map/all_to_all | solution.py:98
  240.6 5.5 %all-to-all-start.10 = ((bf16[16,24,1024]{2,1,0:T(8,128)(2,1)}), bf16[16,24,1024]{2,1,0:T(8,128)(2,1)S(1)}, u32[]{:S(2)}, u32[]{:S(2)}) async-start(bf16[16,24,1024]{2,1,0:T(8,128)(2,1)} %bitcast.259), calls=%async_computation.10 | async-start | bytes 1572864 | tf_op jit(solution)/shard_map/all_to_all | solution.py:90
  246.2 1.4 add_convert_fusion.6
  247.6 1.3 collective-permute-start.2
  249.0 4.9 %collective-permute-done.2 = bf16[32,1024]{1,0:T(8,128)(2,1)S(1)} collective-permute-done((bf16[32,1024]{1,0:T(8,128)(2,1)S(1)}, bf16[32,1024]{1,0:T(8,128)(2,1)S(1)}, u32[]{:S(2)}, u32[]{:S(2)}) %collective-permute-start.2) | collective-permute-done | bytes 65568 | tf_op jit(solution)/shard_map/ppermute | solution.py:12
  254.5 1.3 multiply_convert_fusion
  255.8 9.0 %all-to-all-done.10 = bf16[16,24,1024]{2,1,0:T(8,128)(2,1)S(1)} async-done(((bf16[16,24,1024]{2,1,0:T(8,128)(2,1)}), bf16[16,24,1024]{2,1,0:T(8,128)(2,1)S(1)}, u32[]{:S(2)}, u32[]{:S(2)}) %all-to-all-start.10) | async-done | bytes 786464 | tf_op jit(solution)/shard_map/all_to_all | solution.py:90
  264.8 5.5 %all-to-all-start.9 = ((bf16[16,24,1024]{2,1,0:T(8,128)(2,1)}), bf16[16,24,1024]{2,1,0:T(8,128)(2,1)}, u32[]{:S(2)}, u32[]{:S(2)}) async-start(bf16[16,24,1024]{2,1,0:T(8,128)(2,1)} %bitcast.264), calls=%async_computation.9 | async-start | bytes 1572864 | tf_op jit(solution)/shard_map/all_to_all | solution.py:91
  270.3 1.4 fusion.4
  271.7 1.4 fusion.19
  273.1 16.0 %all-to-all-done.9 = bf16[16,24,1024]{2,1,0:T(8,128)(2,1)} async-done(((bf16[16,24,1024]{2,1,0:T(8,128)(2,1)}), bf16[16,24,1024]{2,1,0:T(8,128)(2,1)}, u32[]{:S(2)}, u32[]{:S(2)}) %all-to-all-start.9) | async-done | bytes 786464 | tf_op jit(solution)/shard_map/all_to_all | solution.py:91
  289.1 1.7 fusion.30
  291.5 1.5 add_convert_fusion.1
  293.0 5.6 %all-to-all-start.11 = ((bf16[16,24,1024]{2,1,0:T(8,128)(2,1)}), bf16[16,24,1024]{2,1,0:T(8,128)(2,1)S(1)}, u32[]{:S(2)}, u32[]{:S(2)}) async-start(bf16[16,24,1024]{2,1,0:T(8,128)(2,1)} %bitcast.48), calls=%async_computation.11 | async-start | bytes 1572864 | tf_op jit(solution)/shard_map/all_to_all | solution.py:98
  298.7 2.0 fusion.46
  300.8 1.8 fusion.47
  302.6 1.8 fusion.48
  304.4 2.7 fusion
  307.1 10.2 %all-to-all-done.11 = bf16[16,24,1024]{2,1,0:T(8,128)(2,1)S(1)} async-done(((bf16[16,24,1024]{2,1,0:T(8,128)(2,1)}), bf16[16,24,1024]{2,1,0:T(8,128)(2,1)S(1)}, u32[]{:S(2)}, u32[]{:S(2)}) %all-to-all-start.11) | async-done | bytes 786464 | tf_op jit(solution)/shard_map/all_to_all | solution.py:98
  317.4 1.1 fusion.61
  (123 shorter events, 14.7 us)
Async XLA Ops:
  0.6 36.8 %copy-start = (bf16[1,1,1024,384]{3,2,1,0:T(8,128)(2,1)S(1)}, bf16[1,1,1024,384]{3,2,1,0:T(8,128)(2,1)}, u32[]{:S(2)}) copy-start(bf16[1,1,1024,384]{3,2,1,0:T(8,128)(2,1)} %param.13) | copy-start | bytes 2359300
  0.6 12.4 %copy-start.29 = (f32[1,4,32,8]{2,3,1,0:T(8,128)S(1)}, f32[1,4,32,8]{2,3,1,0:T(8,128)}, u32[]{:S(2)}) copy-start(f32[1,4,32,8]{2,3,1,0:T(8,128)} %param.12) | copy-start | bytes 12292
  0.7 13.3 %copy-start.8 = (bf16[4,32,1024]{2,1,0:T(8,128)(2,1)S(1)}, bf16[4,32,1024]{2,1,0:T(8,128)(2,1)}, u32[]{:S(2)}) copy-start(bf16[4,32,1024]{2,1,0:T(8,128)(2,1)} %param.10) | copy-start | bytes 786436
  0.7 13.3 %copy-start.20 = (bf16[1,32,1024]{2,1,0:T(8,128)(2,1)S(1)}, bf16[1,32,1024]{2,1,0:T(8,128)(2,1)}, u32[]{:S(2)}) copy-start(bf16[1,32,1024]{2,1,0:T(8,128)(2,1)} %param.9) | copy-start | bytes 196612
  5.7 26.1 %all-to-all-start.1 = ((bf16[16,24,1024]{2,1,0:T(8,128)(2,1)}), bf16[16,24,1024]{2,1,0:T(8,128)(2,1)S(1)}, u32[]{:S(2)}, u32[]{:S(2)}) async-start(bf16[16,24,1024]{2,1,0:T(8,128)(2,1)} %bitcast.8), calls=%async_computation.1 | async-start | bytes 1572864 | tf_op jit(solution)/shard_map/all_to_all | solution.py:90
  31.8 7.1 %copy-start.2 = (bf16[1,1,1024,384]{3,2,1,0:T(8,128)(2,1)S(1)}, bf16[1,1,1024,384]{3,2,1,0:T(8,128)(2,1)}, u32[]{:S(2)}) copy-start(bf16[1,1,1024,384]{3,2,1,0:T(8,128)(2,1)} %param.14) | copy-start | bytes 2359300
  31.8 24.4 %all-to-all-start = ((bf16[16,24,1024]{2,1,0:T(8,128)(2,1)}), bf16[16,24,1024]{2,1,0:T(8,128)(2,1)}, u32[]{:S(2)}, u32[]{:S(2)}) async-start(bf16[16,24,1024]{2,1,0:T(8,128)(2,1)} %bitcast.4), calls=%async_computation | async-start | bytes 1572864 | tf_op jit(solution)/shard_map/all_to_all | solution.py:91
  38.9 17.3 %copy-start.1 = (bf16[1,1,384,1024]{3,2,1,0:T(8,128)(2,1)S(1)}, bf16[1,1,384,1024]{3,2,1,0:T(8,128)(2,1)}, u32[]{:S(2)}) copy-start(bf16[1,1,384,1024]{3,2,1,0:T(8,128)(2,1)} %param.15) | copy-start | bytes 2359300
  40.3 17.8 %copy-start.9 = (f32[384,384]{1,0:T(8,128)S(1)}, f32[384,384]{1,0:T(8,128)}, u32[]{:S(2)}) copy-start(f32[384,384]{1,0:T(8,128)} %fusion.16) | copy-start | bytes 1769476
  56.2 1.8 copy-start.11
  60.2 24.2 %all-to-all-start.2 = ((bf16[16,24,1024]{2,1,0:T(8,128)(2,1)}), bf16[16,24,1024]{2,1,0:T(8,128)(2,1)S(1)}, u32[]{:S(2)}, u32[]{:S(2)}) async-start(bf16[16,24,1024]{2,1,0:T(8,128)(2,1)} %bitcast.266), calls=%async_computation.2 | async-start | bytes 1572864 | tf_op jit(solution)/shard_map/all_to_all | solution.py:98
  84.4 0.9 copy-start.5
  85.3 24.2 %all-to-all-start.4 = ((bf16[16,24,1024]{2,1,0:T(8,128)(2,1)}), bf16[16,24,1024]{2,1,0:T(8,128)(2,1)S(1)}, u32[]{:S(2)}, u32[]{:S(2)}) async-start(bf16[16,24,1024]{2,1,0:T(8,128)(2,1)} %bitcast.261), calls=%async_computation.4 | async-start | bytes 1572864 | tf_op jit(solution)/shard_map/all_to_all | solution.py:90
  92.9 1.3 copy-start.23
  92.9 6.3 %collective-permute-start = (bf16[32,1024]{1,0:T(8,128)(2,1)S(1)}, bf16[32,1024]{1,0:T(8,128)(2,1)S(1)}, u32[]{:S(2)}, u32[]{:S(2)}) collective-permute-start(bf16[32,1024]{1,0:T(8,128)(2,1)S(1)} %fusion.1), channel_id=1, source_target_pairs={{16,0},{17,1},{18,2},{19,3},{20,4},{21,5},{22,6},{23,7},{24,8},{25... | collective-permute-start | bytes 196616 | tf_op jit(solution)/shard_map/ppermute | solution.py:12
  109.5 24.3 %all-to-all-start.3 = ((bf16[16,24,1024]{2,1,0:T(8,128)(2,1)}), bf16[16,24,1024]{2,1,0:T(8,128)(2,1)}, u32[]{:S(2)}, u32[]{:S(2)}) async-start(bf16[16,24,1024]{2,1,0:T(8,128)(2,1)} %bitcast.262), calls=%async_computation.3 | async-start | bytes 1572864 | tf_op jit(solution)/shard_map/all_to_all | solution.py:91
  117.8 17.8 %copy-start.12 = (f32[384,384]{1,0:T(8,128)S(1)}, f32[384,384]{1,0:T(8,128)}, u32[]{:S(2)}) copy-start(f32[384,384]{1,0:T(8,128)} %fusion.12) | copy-start | bytes 1769476
  133.8 1.8 copy-start.14
  137.8 5.6 %copy-start.30 = (s32[1,1,32,8]{2,3,1,0:T(8,128)S(1)}, s32[1,1,32,8]{2,3,1,0:T(8,128)}, u32[]{:S(2)}) copy-start(s32[1,1,32,8]{2,3,1,0:T(8,128)} %get-tuple-element.7) | copy-start | bytes 3076
  137.8 24.3 %all-to-all-start.5 = ((bf16[16,24,1024]{2,1,0:T(8,128)(2,1)}), bf16[16,24,1024]{2,1,0:T(8,128)(2,1)S(1)}, u32[]{:S(2)}, u32[]{:S(2)}) async-start(bf16[16,24,1024]{2,1,0:T(8,128)(2,1)} %bitcast.267), calls=%async_computation.5 | async-start | bytes 1572864 | tf_op jit(solution)/shard_map/all_to_all | solution.py:98
  162.1 0.9 copy-start.4
  163.0 24.2 %all-to-all-start.7 = ((bf16[16,24,1024]{2,1,0:T(8,128)(2,1)}), bf16[16,24,1024]{2,1,0:T(8,128)(2,1)S(1)}, u32[]{:S(2)}, u32[]{:S(2)}) async-start(bf16[16,24,1024]{2,1,0:T(8,128)(2,1)} %bitcast.260), calls=%async_computation.7 | async-start | bytes 1572864 | tf_op jit(solution)/shard_map/all_to_all | solution.py:90
  170.6 1.3 copy-start.25
  170.6 6.3 %collective-permute-start.1 = (bf16[32,1024]{1,0:T(8,128)(2,1)S(1)}, bf16[32,1024]{1,0:T(8,128)(2,1)S(1)}, u32[]{:S(2)}, u32[]{:S(2)}) collective-permute-start(bf16[32,1024]{1,0:T(8,128)(2,1)S(1)} %add_convert_fusion.7), channel_id=1, source_target_pairs={{16,0},{17,1},{18,2},{19,3},{20,4},{21,5},{22,6},{23,7},{24,8},{25... | collective-permute-start | bytes 196616 | tf_op jit(solution)/shard_map/ppermute | solution.py:12
  187.2 24.3 %all-to-all-start.6 = ((bf16[16,24,1024]{2,1,0:T(8,128)(2,1)}), bf16[16,24,1024]{2,1,0:T(8,128)(2,1)}, u32[]{:S(2)}, u32[]{:S(2)}) async-start(bf16[16,24,1024]{2,1,0:T(8,128)(2,1)} %bitcast.263), calls=%async_computation.6 | async-start | bytes 1572864 | tf_op jit(solution)/shard_map/all_to_all | solution.py:91
  195.6 17.7 %copy-start.16 = (f32[384,384]{1,0:T(8,128)S(1)}, f32[384,384]{1,0:T(8,128)}, u32[]{:S(2)}) copy-start(f32[384,384]{1,0:T(8,128)} %fusion.8) | copy-start | bytes 1769476
  211.5 1.8 copy-start.18
  215.5 24.2 %all-to-all-start.8 = ((bf16[16,24,1024]{2,1,0:T(8,128)(2,1)}), bf16[16,24,1024]{2,1,0:T(8,128)(2,1)S(1)}, u32[]{:S(2)}, u32[]{:S(2)}) async-start(bf16[16,24,1024]{2,1,0:T(8,128)(2,1)} %bitcast.265), calls=%async_computation.8 | async-start | bytes 1572864 | tf_op jit(solution)/shard_map/all_to_all | solution.py:98
  239.7 0.9 copy-start.3
  240.6 24.2 %all-to-all-start.10 = ((bf16[16,24,1024]{2,1,0:T(8,128)(2,1)}), bf16[16,24,1024]{2,1,0:T(8,128)(2,1)S(1)}, u32[]{:S(2)}, u32[]{:S(2)}) async-start(bf16[16,24,1024]{2,1,0:T(8,128)(2,1)} %bitcast.259), calls=%async_computation.10 | async-start | bytes 1572864 | tf_op jit(solution)/shard_map/all_to_all | solution.py:90
  247.5 1.3 copy-start.27
  247.6 6.3 %collective-permute-start.2 = (bf16[32,1024]{1,0:T(8,128)(2,1)S(1)}, bf16[32,1024]{1,0:T(8,128)(2,1)S(1)}, u32[]{:S(2)}, u32[]{:S(2)}) collective-permute-start(bf16[32,1024]{1,0:T(8,128)(2,1)S(1)} %add_convert_fusion.6), channel_id=1, source_target_pairs={{16,0},{17,1},{18,2},{19,3},{20,4},{21,5},{22,6},{23,7},{24,8},{25... | collective-permute-start | bytes 196616 | tf_op jit(solution)/shard_map/ppermute | solution.py:12
  253.9 0.6 copy-start.21
  264.8 24.3 %all-to-all-start.9 = ((bf16[16,24,1024]{2,1,0:T(8,128)(2,1)}), bf16[16,24,1024]{2,1,0:T(8,128)(2,1)}, u32[]{:S(2)}, u32[]{:S(2)}) async-start(bf16[16,24,1024]{2,1,0:T(8,128)(2,1)} %bitcast.264), calls=%async_computation.9 | async-start | bytes 1572864 | tf_op jit(solution)/shard_map/all_to_all | solution.py:91
  273.1 17.7 %copy-start.6 = (f32[384,384]{1,0:T(8,128)S(1)}, f32[384,384]{1,0:T(8,128)}, u32[]{:S(2)}) copy-start(f32[384,384]{1,0:T(8,128)} %fusion.4) | copy-start | bytes 1769476
  273.1 17.7 %copy-start.7 = (f32[384,384]{1,0:T(8,128)S(1)}, f32[384,384]{1,0:T(8,128)}, u32[]{:S(2)}) copy-start(f32[384,384]{1,0:T(8,128)} %fusion.19) | copy-start | bytes 1769476
  293.0 5.6 %copy-start.10 = (f32[384,384]{1,0:T(8,128)S(1)}, f32[384,384]{1,0:T(8,128)}, u32[]{:S(2)}) copy-start(f32[384,384]{1,0:T(8,128)} %fusion.16) | copy-start | bytes 1769476
  293.0 24.3 %all-to-all-start.11 = ((bf16[16,24,1024]{2,1,0:T(8,128)(2,1)}), bf16[16,24,1024]{2,1,0:T(8,128)(2,1)S(1)}, u32[]{:S(2)}, u32[]{:S(2)}) async-start(bf16[16,24,1024]{2,1,0:T(8,128)(2,1)} %bitcast.48), calls=%async_computation.11 | async-start | bytes 1572864 | tf_op jit(solution)/shard_map/all_to_all | solution.py:98
  298.7 2.1 copy-start.13
  298.7 2.1 copy-start.15
  300.7 1.9 copy-start.17
  300.8 1.9 copy-start.19
  304.4 13.0 %copy-start.22 = (bf16[32,1024]{1,0:T(8,128)(2,1)S(1)}, bf16[32,1024]{1,0:T(8,128)(2,1)}, u32[]{:S(2)}) copy-start(bf16[32,1024]{1,0:T(8,128)(2,1)} %copy-done.21) | copy-start | bytes 196612
  304.4 14.1 %copy-start.24 = (bf16[32,1024]{1,0:T(8,128)(2,1)S(1)}, bf16[32,1024]{1,0:T(8,128)(2,1)}, u32[]{:S(2)}) copy-start(bf16[32,1024]{1,0:T(8,128)(2,1)} %copy-done.23) | copy-start | bytes 196612
  304.4 14.1 %copy-start.26 = (bf16[32,1024]{1,0:T(8,128)(2,1)S(1)}, bf16[32,1024]{1,0:T(8,128)(2,1)}, u32[]{:S(2)}) copy-start(bf16[32,1024]{1,0:T(8,128)(2,1)} %copy-done.25) | copy-start | bytes 196612
  304.4 14.1 %copy-start.28 = (bf16[32,1024]{1,0:T(8,128)(2,1)S(1)}, bf16[32,1024]{1,0:T(8,128)(2,1)}, u32[]{:S(2)}) copy-start(bf16[32,1024]{1,0:T(8,128)(2,1)} %copy-done.27) | copy-start | bytes 196612
where the time goes:
time: 321 us; the launch traced here: 319 us
  waiting for transfers between devices  177 us (55%)
  starting transfers between devices  72.1 us (22%)
  matrix products  54.4 us (17%)
  local copies, waits for them, and re-layouts  9.15 us (3%)
  other arithmetic  5.07 us (2%)
    all_to_all x4, waiting for transfers between devices, per_device(): lax.all_to_all(grad_rows, 'expert', split_axis=0, concat_axis=0, tiled=True)  63.9 us
    all_to_all x4, waiting for transfers between devices, per_device(): lax.all_to_all(row_grad.reshape(experts, slot_rows, width), 'expert', spl...  55.4 us
    all_to_all x4, waiting for transfers between devices, per_device(): lax.all_to_all(input_rows, 'expert', split_axis=0, concat_axis=0, tiled=T...  43.4 us
    all_to_all x4, starting transfers between devices, per_device(): lax.all_to_all(input_rows, 'expert', split_axis=0, concat_axis=0, tiled=T...  23.8 us
    all_to_all x4, starting transfers between devices, per_device(): lax.all_to_all(grad_rows, 'expert', split_axis=0, concat_axis=0, tiled=True)  22.2 us
    all_to_all x4, starting transfers between devices, per_device(): lax.all_to_all(row_grad.reshape(experts, slot_rows, width), 'expert', spl...  22.2 us
    ppermute x3, waiting for transfers between devices, passed_along(): lax.ppermute(value, axis, [(source, source + steps) for source in range(l...  14.6 us
    dot_general x8, matrix products, select_rows(): return jnp.dot(select, source, preferred_element_type=jnp.float32)  13.8 us
  transfers between devices with their start and end apart: 15, of which 15 were waited for; matrix products, arithmetic and copies ran while one was open for 13% of the time, Pallas kernels for 0%

commit v1 on v0

v1 whole, which is shorter than its diff:
```python
import jax
import jax.numpy as jnp
from jax import lax
from jax.sharding import PartitionSpec as P


def passed_along(value, axis, steps):
    count = lax.axis_size(axis)
    leading, last = (max(0, -steps), min(count, count - steps))
    return lax.ppermute(value, axis, [(source, source + steps) for source in range(leading, last)])


def per_device(acts, carried, loss_grad, expert_ids, probs, w_gate, w_up, w_down):
    experts = lax.axis_size("expert")
    ticks, tokens, width = acts.shape[1:]
    gate_weight, up_weight, down_weight = w_gate[0, 0], w_up[0, 0], w_down[0, 0]
    is_last = lax.axis_index("section") == lax.axis_size("section") - 1
    me = lax.axis_index("expert")
    hit = expert_ids[0][..., None] == jnp.arange(experts, dtype=jnp.int32)
    routed = jnp.sum(jnp.where(hit, probs[0][..., None], 0.0), axis=2)
    routed = lax.all_gather(routed, "expert", axis=1, tiled=True)
    mine = jnp.arange(experts, dtype=jnp.int32) == me
    weight = jnp.sum(jnp.where(mine, routed, 0.0), axis=2)
    contract = (((1,), (1,)), ((), ()))
    rows_contract = (((0,), (0,)), ((), ()))
    incoming = jnp.where(is_last, loss_grad[0], carried[0])
    rows = lax.all_gather(acts[0], "expert", axis=1, tiled=True)
    results = []
    down_sum = jnp.zeros(down_weight.shape, jnp.float32)
    for moment in range(ticks):
        gate_pre = jnp.dot(rows[moment], gate_weight, preferred_element_type=jnp.float32)
        up_pre = jnp.dot(rows[moment], up_weight, preferred_element_type=jnp.float32)
        sigma = jax.nn.sigmoid(gate_pre)
        active = gate_pre * sigma
        hidden = (active * up_pre).astype(jnp.bfloat16)
        gathered = lax.all_gather(incoming, "expert", axis=0, tiled=True)
        grad = (gathered.astype(jnp.float32) * weight[moment][:, None]).astype(jnp.bfloat16)
        hidden_grad = lax.dot_general(grad, down_weight, contract, preferred_element_type=jnp.float32)
        gate_grad = (hidden_grad * up_pre * sigma * (1.0 + gate_pre * (1.0 - sigma))).astype(jnp.bfloat16)
        up_grad = (hidden_grad * active).astype(jnp.bfloat16)
        row_grad = lax.dot_general(gate_grad, gate_weight, contract, preferred_element_type=jnp.float32)
        row_grad = row_grad + lax.dot_general(up_grad, up_weight, contract, preferred_element_type=jnp.float32)
        back = lax.psum_scatter(row_grad.astype(jnp.bfloat16), "expert", scatter_dimension=0, tiled=True)
        result = (incoming.astype(jnp.float32) + back.astype(jnp.float32)).astype(jnp.bfloat16)
        results.append(result)
        down_sum = down_sum + lax.dot_general(hidden, grad, rows_contract, preferred_element_type=jnp.float32)
        if moment + 1 < ticks:
            arriving = passed_along(result, "section", -1)
            incoming = jnp.where(is_last, loss_grad[moment + 1], arriving)
    out_grad = jnp.stack(results, axis=0)[None]
    return (out_grad, down_sum.astype(jnp.bfloat16)[None, None])


def solution(mesh):
    return jax.shard_map(
        per_device,
        mesh=mesh,
        in_specs=(
            P("section", None, "expert", None),
            P("section", "expert", None),
            P(None, "expert", None),
            P("section", None, "expert", None),
            P("section", None, "expert", None),
            P("section", "expert", None, None),
            P("section", "expert", None, None),
            P("section", "expert", None, None),
        ),
        out_specs=(P("section", None, "expert", None), P("section", "expert", None, None)),
        check_vma=False,
    )
```

time: 321 us -> 493 us (1.54)
  waiting for transfers between devices: 177 us -> 389 us
  starting transfers between devices: 72.1 us -> 4.42 us
  blocking collectives: 0 us -> 26.3 us
  between operations: 1.3 us -> 14.2 us
  matrix products: 54.4 us -> 45.6 us
  local copies, waits for them, and re-layouts: 9.15 us -> 3.94 us
    reduce_scatter x0 -> x4, waiting for transfers between devices: none -> 218 us  [per_device(): lax.psum_scatter(row_grad.astype(jnp.bfloat16), 'expert', scatter_dimensi...]
    all_to_all x12 -> x0, waiting for transfers between devices: 163 us -> none  [the longest x4 63.9 us: per_device(): lax.all_to_all(grad_rows, 'expert', split_axis=0, concat_axis=0, tiled=True)]
    all_gather x0 -> x5, waiting for transfers between devices: none -> 155 us  [the longest x4 107 us: per_device(): gathered = lax.all_gather(incoming, 'expert', axis=0, tiled=True)]
    all_to_all x12 -> x0, starting transfers between devices: 68.2 us -> none  [the longest x4 23.8 us: per_device(): lax.all_to_all(input_rows, 'expert', split_axis=0, concat_axis=0, tiled=T...]
    all_gather x0 -> x1, blocking collectives: none -> 26.3 us  [per_device(): routed = lax.all_gather(routed, 'expert', axis=1, tiled=True)]
    dot_general x36 -> x24, matrix products: 54.4 us -> 45.6 us  [the longest x4 10.5 us: per_device(): jnp.dot(rows[moment], up_weight, preferred_element_type=jnp.float32)]
  transfers between devices with their start and end apart: 15 -> 12, of which waited for: 15 -> 12; matrix products, arithmetic and copies ran while one was open for 13% -> 5% of each run, Pallas kernels for 0% -> 0%
where the time goes in v1:
time: 493 us; the launch traced here: 492 us
  waiting for transfers between devices  389 us (79%)
  matrix products  45.6 us (9%)
  blocking collectives  26.3 us (5%)
  between operations  14.2 us (3%)
  other arithmetic  9.07 us (2%)
    reduce_scatter x4, waiting for transfers between devices, per_device(): lax.psum_scatter(row_grad.astype(jnp.bfloat16), 'expert', scatter_dimensi...  218 us
    all_gather x4, waiting for transfers between devices, per_device(): gathered = lax.all_gather(incoming, 'expert', axis=0, tiled=True)  107 us
    all_gather x1, waiting for transfers between devices, per_device(): rows = lax.all_gather(acts[0], 'expert', axis=1, tiled=True)  48.9 us
    all_gather x1, blocking collectives, per_device(): routed = lax.all_gather(routed, 'expert', axis=1, tiled=True)  26.3 us
    ppermute x3, waiting for transfers between devices, passed_along(): lax.ppermute(value, axis, [(source, source + steps) for source in range(l...  14.6 us
    dot_general x4, matrix products, per_device(): jnp.dot(rows[moment], up_weight, preferred_element_type=jnp.float32)  10.5 us
  transfers between devices with their start and end apart: 12, of which 12 were waited for; matrix products, arithmetic and copies ran while one was open for 5% of the time, Pallas kernels for 0%

profile of v1, /device:TPU:0, one launch (start us, length us, event | category | flops | bytes accessed | tf_op | source)
XLA Modules:
  0.0 492.3 jit_solution(8581582296624763628)
XLA Ops:
  7.2 1.6 slice_select_fusion
  8.9 0.7 all-gather.16.cloned.1.call-update
  9.6 0.8 select_reduce_fusion.1
  10.5 26.3 %all_gather.19 = f32[4,512,16]{2,0,1:T(4,128)S(1)} all-gather(f32[4,32,16]{2,0,1:T(4,128)S(1)} %copy.12), channel_id=1, replica_groups=mesh['section'=2,'expert'=16] {'expert'}, dimensions={1}, use_global_device_ids=true | all-gather | bytes 139264 | tf_op jit(solution)/shard_map/all_gather | solution.py:21
  36.8 0.6 select_reduce_fusion
  37.4 0.3 fusion.73
  37.7 0.1 copy.15
  37.8 14.5 %all-gather.14.cloned.1.call-done = bf16[1,512,1024]{2,1,0:T(8,128)(2,1)} async-done(((bf16[1,32,1024]{2,1,0:T(8,128)(2,1)}), bf16[1,512,1024]{2,1,0:T(8,128)(2,1)}) %all-gather.14.cloned.1.call-update) | async-done | bytes 1048592 | tf_op jit(solution)/shard_map/all_gather | solution.py:36
  52.3 2.9 fusion.36
  55.1 48.9 %all-gather.16.cloned.1.call-done = bf16[1,4,512,1024]{3,2,1,0:T(8,128)(2,1)} async-done(((bf16[1,4,32,1024]{3,2,1,0:T(8,128)(2,1)}), bf16[1,4,512,1024]{3,2,1,0:T(8,128)(2,1)}) %all-gather.16.cloned.1.call-update) | async-done | bytes 4194320 | tf_op jit(solution)/shard_map/all_gather | solution.py:27
  104.0 2.0 fusion.2
  106.0 2.2 fusion.3
  108.3 0.9 copy-done.20
  109.2 0.9 fusion.19
  110.1 1.8 add_convert_fusion.3
  111.9 56.0 %reduce-scatter.5.cloned.1.call-done = bf16[32,1024]{1,0:T(8,128)(2,1)} async-done(((bf16[512,1024]{1,0:T(8,128)(2,1)}), bf16[32,1024]{1,0:T(8,128)(2,1)}) %reduce-scatter.5.cloned.1.call-update) | async-done | bytes 65552 | tf_op jit(solution)/shard_map/reduce_scatter | solution.py:43
  168.0 0.9 fusion.59
  168.8 1.3 collective-permute-start
  170.1 4.9 collective-permute-done
  175.0 0.6 bitcast_select_fusion.2
  175.7 0.1 copy.16
  175.8 2.8 fusion.4
  178.7 3.0 fusion.5
  181.7 30.2 %all-gather.8.cloned.1.call-done = bf16[512,1024]{1,0:T(8,128)(2,1)} async-done(((bf16[32,1024]{1,0:T(8,128)(2,1)}), bf16[512,1024]{1,0:T(8,128)(2,1)}) %all-gather.8.cloned.1.call-update) | async-done | bytes 1048592 | tf_op jit(solution)/shard_map/all_gather | solution.py:36
  211.9 2.1 fusion.34
  214.0 0.9 fusion.16
  214.9 0.3 copy-done.11
  215.1 1.7 add_convert_fusion.2
  216.9 56.4 %reduce-scatter.7.cloned.1.call-done = bf16[32,1024]{1,0:T(8,128)(2,1)} async-done(((bf16[512,1024]{1,0:T(8,128)(2,1)}), bf16[32,1024]{1,0:T(8,128)(2,1)}) %reduce-scatter.7.cloned.1.call-update) | async-done | bytes 65552 | tf_op jit(solution)/shard_map/reduce_scatter | solution.py:43
  273.3 0.9 add_convert_fusion.7
  274.2 1.3 collective-permute-start.1
  275.5 4.9 collective-permute-done.1
  280.3 0.6 bitcast_select_fusion.1
  281.2 2.8 fusion.6
  284.0 3.1 fusion.7
  287.1 30.2 %all-gather.10.cloned.1.call-done = bf16[512,1024]{1,0:T(8,128)(2,1)} async-done(((bf16[32,1024]{1,0:T(8,128)(2,1)}), bf16[512,1024]{1,0:T(8,128)(2,1)}) %all-gather.10.cloned.1.call-update) | async-done | bytes 1048592 | tf_op jit(solution)/shard_map/all_gather | solution.py:36
  317.2 2.1 fusion.32
  319.3 0.9 fusion.13
  320.2 0.3 copy-done.12
  320.5 1.8 add_convert_fusion.1
  322.4 56.4 %reduce-scatter.9.cloned.1.call-done = bf16[32,1024]{1,0:T(8,128)(2,1)} async-done(((bf16[512,1024]{1,0:T(8,128)(2,1)}), bf16[32,1024]{1,0:T(8,128)(2,1)}) %reduce-scatter.9.cloned.1.call-update) | async-done | bytes 65552 | tf_op jit(solution)/shard_map/reduce_scatter | solution.py:43
  378.8 0.9 add_convert_fusion.6
  379.6 1.3 collective-permute-start.2
  380.9 4.9 collective-permute-done.2
  385.8 0.6 bitcast_select_fusion
  386.5 0.2 reduce-scatter.11.cloned.1.call-start
  386.8 1.9 fusion.8
  388.8 2.2 fusion.9
  390.9 31.8 %all-gather.12.cloned.1.call-done = bf16[512,1024]{1,0:T(8,128)(2,1)} async-done(((bf16[32,1024]{1,0:T(8,128)(2,1)}), bf16[512,1024]{1,0:T(8,128)(2,1)}) %all-gather.12.cloned.1.call-update) | async-done | bytes 1048592 | tf_op jit(solution)/shard_map/all_gather | solution.py:36
  422.7 2.2 fusion.30
  424.9 0.8 fusion.10
  425.7 0.3 copy-done.13
  426.0 1.7 add_convert_fusion
  427.8 2.6 fusion.44
  430.5 0.8 fusion.42
  431.3 0.4 copy-done.8
  431.7 0.2 copy-done.18
  431.9 0.2 copy-done.24
  432.1 0.8 fusion.43
  432.9 0.4 copy-done.1
  433.4 1.7 fusion.1
  435.1 49.1 %reduce-scatter.11.cloned.1.call-done = bf16[32,1024]{1,0:T(8,128)(2,1)} async-done(((bf16[512,1024]{1,0:T(8,128)(2,1)}), bf16[32,1024]{1,0:T(8,128)(2,1)}) %reduce-scatter.11.cloned.1.call-update) | async-done | bytes 65552 | tf_op jit(solution)/shard_map/reduce_scatter | solution.py:43
  484.2 0.9 fusion.60
  485.0 0.7 maximum_bitcast_fusion
  (62 shorter events, 0.9 us)
Async XLA Ops:
  7.2 96.8 %copy-start = (bf16[1,1,1024,384]{3,2,1,0:T(8,128)(2,1)S(1)}, bf16[1,1,1024,384]{3,2,1,0:T(8,128)(2,1)}, u32[]{:S(2)}) copy-start(bf16[1,1,1024,384]{3,2,1,0:T(8,128)(2,1)} %param.13) | copy-start | bytes 2359300
  7.2 45.1 %all-gather.14.cloned.1.call-start = ((), (), s32[]{:S(2)}) async-start(), calls=%async_computation.11 | async-start | bytes 1114112 | tf_op jit(solution)/shard_map/all_gather | solution.py:36
  8.8 95.2 %all-gather.16.cloned.1.call-start = ((), (), s32[]{:S(2)}) async-start(), calls=%async_computation.12 | async-start | bytes 4456448 | tf_op jit(solution)/shard_map/all_gather | solution.py:27
  9.6 158.4 %reduce-scatter.5.cloned.1.call-start = ((), (), s32[]{:S(2)}) async-start(), calls=%async_computation.4 | async-start | bytes 1114112 | tf_op jit(solution)/shard_map/reduce_scatter | solution.py:43
  36.8 15.5 %copy-start.9 = (bf16[1,1,384,1024]{3,2,1,0:T(8,128)(2,1)S(1)}, bf16[1,1,384,1024]{3,2,1,0:T(8,128)(2,1)}, u32[]{:S(2)}) copy-start(bf16[1,1,384,1024]{3,2,1,0:T(8,128)(2,1)} %param.15) | copy-start | bytes 2359300
  104.0 2.0 copy-start.10
  106.0 4.1 copy-start.14
  106.0 3.2 copy-start.19
  108.3 0.9 copy-start.20
  110.1 57.9 %copy-start.2 = (bf16[1,32,1024]{2,1,0:T(8,128)(2,1)S(1)}, bf16[1,32,1024]{2,1,0:T(8,128)(2,1)}, u32[]{:S(2)}) copy-start(bf16[1,32,1024]{2,1,0:T(8,128)(2,1)} %slice_select_fusion) | copy-start | bytes 196612
  110.1 64.9 %copy-start.6 = (bf16[4,32,1024]{2,1,0:T(8,128)(2,1)S(1)}, bf16[4,32,1024]{2,1,0:T(8,128)(2,1)}, u32[]{:S(2)}) copy-start(bf16[4,32,1024]{2,1,0:T(8,128)(2,1)} %param.10) | copy-start | bytes 786436
  111.9 100.0 %all-gather.8.cloned.1.call-start = ((), (), s32[]{:S(2)}) async-start(), calls=%async_computation.5 | async-start | bytes 1114112 | tf_op jit(solution)/shard_map/all_gather | solution.py:36
  168.8 6.2 %collective-permute-start = (bf16[32,1024]{1,0:T(8,128)(2,1)S(1)}, bf16[32,1024]{1,0:T(8,128)(2,1)S(1)}, u32[]{:S(2)}, u32[]{:S(2)}) collective-permute-start(bf16[32,1024]{1,0:T(8,128)(2,1)S(1)} %fusion.59), channel_id=1, source_target_pairs={{16,0},{17,1},{18,2},{19,3},{20,4},{21,5},{22,6},{23,7},{24,8},{25... | collective-permute-start | bytes 196616 | tf_op jit(solution)/shard_map/ppermute | solution.py:10
  175.7 97.7 %reduce-scatter.7.cloned.1.call-start = ((), (), s32[]{:S(2)}) async-start(), calls=%async_computation.6 | async-start | bytes 1114112 | tf_op jit(solution)/shard_map/reduce_scatter | solution.py:43
  211.9 2.1 copy-start.15
  211.9 2.1 copy-start.21
  214.0 1.1 copy-start.11
  215.1 58.2 %copy-start.4 = (bf16[32,1024]{1,0:T(8,128)(2,1)S(1)}, bf16[32,1024]{1,0:T(8,128)(2,1)}, u32[]{:S(2)}) copy-start(bf16[32,1024]{1,0:T(8,128)(2,1)} %bitcast_select_fusion.2) | copy-start | bytes 196612
  216.9 100.3 %all-gather.10.cloned.1.call-start = ((), (), s32[]{:S(2)}) async-start(), calls=%async_computation.7 | async-start | bytes 1114112 | tf_op jit(solution)/shard_map/all_gather | solution.py:36
  274.2 6.2 %collective-permute-start.1 = (bf16[32,1024]{1,0:T(8,128)(2,1)S(1)}, bf16[32,1024]{1,0:T(8,128)(2,1)S(1)}, u32[]{:S(2)}, u32[]{:S(2)}) collective-permute-start(bf16[32,1024]{1,0:T(8,128)(2,1)S(1)} %add_convert_fusion.7), channel_id=1, source_target_pairs={{16,0},{17,1},{18,2},{19,3},{20,4},{21,5},{22,6},{23,7},{24,8},{25... | collective-permute-start | bytes 196616 | tf_op jit(solution)/shard_map/ppermute | solution.py:10
  281.0 97.8 %reduce-scatter.9.cloned.1.call-start = ((), (), s32[]{:S(2)}) async-start(), calls=%async_computation.8 | async-start | bytes 1114112 | tf_op jit(solution)/shard_map/reduce_scatter | solution.py:43
  317.2 2.1 copy-start.17
  317.2 2.1 copy-start.23
  319.3 1.1 copy-start.12
  320.5 58.3 %copy-start.5 = (bf16[32,1024]{1,0:T(8,128)(2,1)S(1)}, bf16[32,1024]{1,0:T(8,128)(2,1)}, u32[]{:S(2)}) copy-start(bf16[32,1024]{1,0:T(8,128)(2,1)} %bitcast_select_fusion.1) | copy-start | bytes 196612
  322.3 100.3 %all-gather.12.cloned.1.call-start = ((), (), s32[]{:S(2)}) async-start(), calls=%async_computation.9 | async-start | bytes 1114112 | tf_op jit(solution)/shard_map/all_gather | solution.py:36
  379.6 6.2 %collective-permute-start.2 = (bf16[32,1024]{1,0:T(8,128)(2,1)S(1)}, bf16[32,1024]{1,0:T(8,128)(2,1)S(1)}, u32[]{:S(2)}, u32[]{:S(2)}) collective-permute-start(bf16[32,1024]{1,0:T(8,128)(2,1)S(1)} %add_convert_fusion.6), channel_id=1, source_target_pairs={{16,0},{17,1},{18,2},{19,3},{20,4},{21,5},{22,6},{23,7},{24,8},{25... | collective-permute-start | bytes 196616 | tf_op jit(solution)/shard_map/ppermute | solution.py:10
  386.5 97.7 %reduce-scatter.11.cloned.1.call-start = ((), (), s32[]{:S(2)}) async-start(), calls=%async_computation.10 | async-start | bytes 1114112 | tf_op jit(solution)/shard_map/reduce_scatter | solution.py:43
  424.9 1.1 copy-start.13
  427.8 2.7 copy-start.7
  427.8 2.7 copy-start.16
  427.8 2.7 copy-start.22
  430.5 1.2 copy-start.8
  430.5 1.4 copy-start.18
  430.5 1.7 copy-start.24
  432.1 1.2 copy-start.1
  433.4 50.8 %copy-start.3 = (bf16[32,1024]{1,0:T(8,128)(2,1)S(1)}, bf16[32,1024]{1,0:T(8,128)(2,1)}, u32[]{:S(2)}) copy-start(bf16[32,1024]{1,0:T(8,128)(2,1)} %bitcast_select_fusion) | copy-start | bytes 196612
Sparse Core Ops, SparseCore 0:
  10.7 41.4 all-gather.13
  54.5 49.4 all-gather.15
  112.0 55.9 reduce-scatter.4
  175.8 36.0 all-gather.7
  217.0 56.2 reduce-scatter.6
  281.1 36.0 all-gather.9
  322.5 56.2 reduce-scatter.8
  386.6 36.0 all-gather.11
  427.9 56.2 reduce-scatter.10

commit v2 on v1

v2 whole, which is shorter than its diff:
```python
import functools

import jax
import jax.numpy as jnp
from jax import lax
from jax.experimental import pallas as pl
from jax.experimental.pallas import tpu as pltpu
from jax.sharding import PartitionSpec as P

MESH = pl.DeviceIdType.MESH
BF16 = jnp.bfloat16
F32 = jnp.float32


def kernel(
    sections, lines,
    acts_ref, carried_ref, loss_ref, routed_ref, gate_ref, up_ref, down_ref,
    out_ref, down_out_ref,
    acts_all, inc_all, routed_all, wide, wide_t, down_t, chosen, columns,
    steep, active_buf, hidden_buf, grad_buf, total,
    part, core_in, x_out, x_in, z_out, z_in, own_sum,
    ag_send, ag_recv, rs_send, rs_recv, relay_send, relay_recv,
):
    ticks, tokens, width = acts_ref.shape
    ff = gate_ref.shape[1]
    section = lax.axis_index("section")
    me = lax.axis_index("expert")
    a = me // 4
    b = lax.rem(me // 2, 2)
    c = lax.rem(me, 2)
    nb, nc = 1 - b, 1 - c
    g = b * 2 + c
    ng = nb * 2 + c
    x_peer = a * 4 + nb * 2 + c
    core_peer = a * 4 + b * 2 + nc
    is_last = section == sections - 1
    half = 2 * lines * tokens

    def line_at(j):
        return lax.rem(a + j, lines)

    def line_peer(j):
        return line_at(j) * 4 + g

    def line_back(j):
        return lax.rem(a + lines - j, lines)

    def rows_of(kind_buf, t):
        return kind_buf if t is None else kind_buf.at[t]

    def gather_copy(buf, t, kind, index, ref_of, target):
        ref = ref_of(rows_of(buf, t))
        return pltpu.make_async_remote_copy(
            src_ref=ref, dst_ref=ref,
            send_sem=ag_send.at[kind, index], recv_sem=ag_recv.at[kind, index],
            device_id={"expert": target}, device_id_type=MESH,
        )

    def z_copy(buf, t, kind, j):
        return gather_copy(buf, t, kind, j - 1, lambda r: r.at[g, a], line_peer(j))

    def x_copy(buf, t, kind, j):
        return gather_copy(buf, t, kind, lines - 1 + j, lambda r: r.at[g, line_back(j)], x_peer)

    def core_copy(buf, t, kind, i):
        group = g if i == 0 else ng
        return gather_copy(buf, t, kind, 2 * lines - 1 + i, lambda r: r.at[group], core_peer)

    def gather_start(buf, t, kind):
        for j in range(1, lines):
            z_copy(buf, t, kind, j).start()
        x_copy(buf, t, kind, 0).start()

    def gather_lines(buf, t, kind):
        for j in range(1, lines):
            z_copy(buf, t, kind, j).wait_recv()
            x_copy(buf, t, kind, j).start()
        core_copy(buf, t, kind, 0).start()

    def gather_cross(buf, t, kind):
        for j in range(lines):
            x_copy(buf, t, kind, j).wait_recv()
        core_copy(buf, t, kind, 1).start()

    def gather_drain(buf, t, kind):
        for j in range(1, lines):
            z_copy(buf, t, kind, j).wait_send()
        for j in range(lines):
            x_copy(buf, t, kind, j).wait_send()
        for i in range(2):
            core_copy(buf, t, kind, i).wait_send()

    def acts_kind(t):
        return 1 + t

    def inc_kind(t):
        return 1 + ticks + t

    def back_copy(t, index, src, dst, target):
        return pltpu.make_async_remote_copy(
            src_ref=src, dst_ref=dst,
            send_sem=rs_send.at[t, index], recv_sem=rs_recv.at[t, index],
            device_id={"expert": target}, device_id_type=MESH,
        )

    def back_core(t, i):
        group = (nb if i == 0 else b) * 2 + nc
        return back_copy(t, i, part.at[t, group], core_in.at[t, i], core_peer)

    def back_x(t, j):
        return back_copy(t, 2 + j, x_out.at[t, line_at(j)], x_in.at[t, line_at(j)], x_peer)

    def back_z(t, j):
        return back_copy(t, 1 + lines + j, z_out.at[t, j - 1], z_in.at[t, j - 1], line_peer(j))

    def relay(t):
        down_one = lax.rem(section + sections - 1, sections)
        return pltpu.make_async_remote_copy(
            src_ref=out_ref.at[t], dst_ref=inc_all.at[t + 1, g, a],
            send_sem=relay_send.at[t], recv_sem=relay_recv.at[t],
            device_id={"section": down_one}, device_id_type=MESH,
        )

    barrier = pltpu.get_barrier_semaphore()
    for j in range(1, lines):
        pl.semaphore_signal(barrier, inc=1, device_id={"expert": line_peer(j)}, device_id_type=MESH)
    for peer in (x_peer, core_peer):
        pl.semaphore_signal(barrier, inc=1, device_id={"expert": peer}, device_id_type=MESH)
    for step in (1, sections - 1):
        other = lax.rem(section + step, sections)
        pl.semaphore_signal(barrier, inc=1, device_id={"section": other}, device_id_type=MESH)

    acts_all[:, g, a] = acts_ref[...]
    routed_all[g, a] = routed_ref[...]

    @pl.when(is_last)
    def _():
        inc_all[:, g, a] = loss_ref[...]

    @pl.when(jnp.logical_not(is_last))
    def _():
        inc_all[0, g, a] = carried_ref[...]

    pl.semaphore_wait(barrier, lines + 3)

    gather_start(routed_all, None, 0)
    gather_start(acts_all, 0, acts_kind(0))
    gather_start(inc_all, 0, inc_kind(0))
    wide[:, :ff] = gate_ref[...]
    wide[:, ff:] = up_ref[...]
    wide_t[:ff, :] = gate_ref[...].T
    wide_t[ff:, :] = up_ref[...].T
    down_t[...] = down_ref[...].T
    total[...] = jnp.zeros_like(total)
    gather_lines(routed_all, None, 0)
    gather_lines(acts_all, 0, acts_kind(0))
    gather_cross(routed_all, None, 0)
    core_copy(routed_all, None, 0, 0).wait_recv()
    core_copy(routed_all, None, 0, 1).wait_recv()
    experts = 4 * lines
    table = routed_all[...].reshape(experts, experts, ticks * tokens)
    mine = lax.broadcasted_iota(jnp.int32, table.shape, 1) == me
    chosen[...] = jnp.sum(jnp.where(mine, table, 0.0), axis=1)
    for i in range(2):
        columns[i] = chosen[pl.ds(i * 2 * lines, 2 * lines), :].T

    def forward(t, side):
        rows = acts_all[t, pl.ds(side * 2, 2)].reshape(half, width)
        pre = jnp.dot(rows, wide[...], preferred_element_type=F32)
        gate_pre, up_pre = pre[:, :ff], pre[:, ff:]
        sigma = 1.0 / (1.0 + jnp.exp(-gate_pre))
        active = gate_pre * sigma
        hidden_buf[side] = (active * up_pre).astype(BF16)
        steep[side] = up_pre * sigma * (1.0 + gate_pre * (1.0 - sigma))
        active_buf[side] = active

    def backward(t, side):
        scale = columns[side, pl.ds(pl.multiple_of(t * tokens, tokens), tokens), :]
        for p in range(2 * lines):
            block = inc_all[t, side * 2 + p // lines, p % lines].astype(F32)
            grad_buf[side, pl.ds(p * tokens, tokens), :] = (block * scale[:, p : p + 1]).astype(BF16)
        hidden_grad = jnp.dot(grad_buf[side], down_t[...], preferred_element_type=F32)
        both = jnp.concatenate(
            [(hidden_grad * steep[side]).astype(BF16), (hidden_grad * active_buf[side]).astype(BF16)], axis=1
        )
        row_grad = jnp.dot(both, wide_t[...], preferred_element_type=F32)
        part[t, pl.ds(side * 2, 2)] = row_grad.astype(BF16).reshape(2, lines, tokens, width)

    def tick(t, carry):
        more = t + 1 < ticks

        @pl.when(t > 0)
        def _():
            @pl.when(jnp.logical_not(is_last))
            def _():
                relay(t - 1).wait_recv()

            gather_start(inc_all, t, inc_kind(t))

        gather_cross(acts_all, t, acts_kind(t))
        core_copy(acts_all, t, acts_kind(t), 0).wait_recv()
        forward(t, b)
        gather_lines(inc_all, t, inc_kind(t))
        core_copy(acts_all, t, acts_kind(t), 1).wait_recv()
        forward(t, nb)
        core_copy(inc_all, t, inc_kind(t), 0).wait_recv()
        backward(t, b)
        back_core(t, 1).start()
        gather_cross(inc_all, t, inc_kind(t))
        core_copy(inc_all, t, inc_kind(t), 1).wait_recv()

        @pl.when(more)
        def _():
            gather_start(acts_all, t + 1, acts_kind(t + 1))

        backward(t, nb)
        back_core(t, 0).start()
        back_core(t, 0).wait_recv()
        for j in range(lines):
            where = line_at(j)
            pair = part[t, ng, where].astype(F32) + core_in[t, 0, where].astype(F32)
            x_out[t, where] = pair.astype(BF16)
            back_x(t, j).start()

        for i in range(2):
            total[...] += lax.dot_general(
                hidden_buf[i], grad_buf[i], (((0,), (0,)), ((), ())), preferred_element_type=F32
            )

        @pl.when(more)
        def _():
            gather_lines(acts_all, t + 1, acts_kind(t + 1))

        back_core(t, 1).wait_recv()
        for j in list(range(1, lines)) + [0]:
            back_x(t, j).wait_recv()
            where = line_at(j)
            quad = part[t, g, where].astype(F32) + core_in[t, 1, where].astype(F32)
            quad = quad + x_in[t, where].astype(F32)
            if j:
                z_out[t, j - 1] = quad.astype(BF16)
                back_z(t, j).start()
            else:
                own_sum[...] = quad + inc_all[t, g, a].astype(F32)
        result = own_sum[...]
        for j in range(1, lines):
            back_z(t, j).wait_recv()
            result = result + z_in[t, j - 1].astype(F32)
        out_ref[t] = result.astype(BF16)

        @pl.when(jnp.logical_and(more, section > 0))
        def _():
            relay(t).start()

        return carry

    lax.fori_loop(0, ticks, tick, 0)
    down_out_ref[...] = total[...].astype(BF16)
    gather_drain(routed_all, None, 0)

    def drain(t, carry):
        gather_drain(acts_all, t, acts_kind(t))
        gather_drain(inc_all, t, inc_kind(t))
        for i in range(2):
            back_core(t, i).wait_send()
        for j in range(lines):
            back_x(t, j).wait_send()
        for j in range(1, lines):
            back_z(t, j).wait_send()

        @pl.when(jnp.logical_and(t + 1 < ticks, section > 0))
        def _():
            relay(t).wait_send()

        return carry

    lax.fori_loop(0, ticks, drain, 0)


def per_device(acts, carried, loss_grad, expert_ids, probs, w_gate, w_up, w_down):
    sections = lax.axis_size("section")
    experts = lax.axis_size("expert")
    lines = experts // 4
    ticks, tokens, width = acts.shape[1:]
    ff = w_gate.shape[3]
    hit = jnp.arange(experts, dtype=jnp.int32)[:, None, None] == expert_ids.reshape(1, ticks * tokens, -1)
    routed = jnp.sum(jnp.where(hit, probs.reshape(1, ticks * tokens, -1), 0.0), axis=2)
    kinds, hops = 1 + 2 * ticks, 2 * lines + 1
    half = 2 * lines * tokens
    dma = pltpu.SemaphoreType.DMA
    vmem = pltpu.VMEM
    gathered = (ticks, 4, lines, tokens, width)
    out, down = pl.pallas_call(
        functools.partial(kernel, sections, lines),
        out_shape=(
            jax.ShapeDtypeStruct((ticks, tokens, width), BF16),
            jax.ShapeDtypeStruct((ff, width), BF16),
        ),
        in_specs=[pl.BlockSpec(memory_space=vmem)] * 7,
        out_specs=(pl.BlockSpec(memory_space=vmem),) * 2,
        scratch_shapes=[
            vmem(gathered, BF16), vmem(gathered, BF16), vmem((4, lines, experts, ticks * tokens), F32),
            vmem((width, 2 * ff), BF16), vmem((2 * ff, width), BF16), vmem((width, ff), BF16),
            vmem((experts, ticks * tokens), F32), vmem((2, ticks * tokens, 2 * lines), F32),
            vmem((2, half, ff), F32), vmem((2, half, ff), F32), vmem((2, half, ff), BF16),
            vmem((2, half, width), BF16), vmem((ff, width), F32),
            vmem(gathered, BF16), vmem((ticks, 2, lines, tokens, width), BF16),
            vmem((ticks, lines, tokens, width), BF16), vmem((ticks, lines, tokens, width), BF16),
            vmem((ticks, lines - 1, tokens, width), BF16), vmem((ticks, lines - 1, tokens, width), BF16),
            vmem((tokens, width), F32),
            dma((kinds, hops)), dma((kinds, hops)), dma((ticks, 1 + 2 * lines)), dma((ticks, 1 + 2 * lines)),
            dma((ticks,)), dma((ticks,)),
        ],
        compiler_params=pltpu.CompilerParams(
            collective_id=0, has_side_effects=True, vmem_limit_bytes=60 * 1024 * 1024
        ),
        cost_estimate=pl.CostEstimate(
            flops=12 * ticks * experts * tokens * width * ff, bytes_accessed=8 * width * ff, transcendentals=0
        ),
        name="window",
    )(acts[0], carried[0], loss_grad, routed, w_gate[0, 0], w_up[0, 0], w_down[0, 0])
    return out[None], down[None, None]


def solution(mesh):
    return jax.shard_map(
        per_device,
        mesh=mesh,
        in_specs=(
            P("section", None, "expert", None),
            P("section", "expert", None),
            P(None, "expert", None),
            P("section", None, "expert", None),
            P("section", None, "expert", None),
            P("section", "expert", None, None),
            P("section", "expert", None, None),
            P("section", "expert", None, None),
        ),
        out_specs=(P("section", None, "expert", None), P("section", "expert", None, None)),
        check_vma=False,
    )
```

time: 493 us -> 137 us (0.28)
  waiting for transfers between devices: 389 us -> 0 us
  Pallas kernels: 0 us -> 130 us
  matrix products: 45.6 us -> 0 us
  blocking collectives: 26.3 us -> 0 us
  between operations: 14.2 us -> 0.64 us
  other arithmetic: 9.07 us -> 0.62 us
    reduce_scatter x4 -> x0, waiting for transfers between devices: 218 us -> none  [per_device(): lax.psum_scatter(row_grad.astype(jnp.bfloat16), 'expert', scatter_dimensi...]
    all_gather x5 -> x0, waiting for transfers between devices: 155 us -> none  [the longest x4 107 us: per_device(): gathered = lax.all_gather(incoming, 'expert', axis=0, tiled=True)]
    pallas_call x0 -> x1, Pallas kernels: none -> 130 us  [per_device(): pl.pallas_call(functools.partial(kernel, sections, lines), out_shape=(jax...]
    dot_general x24 -> x0, matrix products: 45.6 us -> none  [the longest x4 10.5 us: per_device(): jnp.dot(rows[moment], up_weight, preferred_element_type=jnp.float32)]
    all_gather x1 -> x0, blocking collectives: 26.3 us -> none  [per_device(): routed = lax.all_gather(routed, 'expert', axis=1, tiled=True)]
    ppermute x3 -> x0, waiting for transfers between devices: 14.6 us -> none  [passed_along(): lax.ppermute(value, axis, [(source, source + steps) for source in range(l...]
  transfers between devices with their start and end apart: 12 -> 0, of which waited for: 12 -> 0; matrix products, arithmetic and copies ran while one was open for 5% -> 0% of each run, Pallas kernels for 0% -> 0%
where the time goes in v2:
time: 137 us; the launch traced here: 136 us
  Pallas kernels  130 us (95%)
  local copies, waits for them, and re-layouts  5.26 us (4%)
    pallas_call x1, Pallas kernels, per_device(): pl.pallas_call(functools.partial(kernel, sections, lines), out_shape=(jax...  130 us
    unnamed x6, local copies, waits for them, and re-layouts  5.1 us

profile of v2, /device:TPU:0, one launch (start us, length us, event | category | flops | bytes accessed | tf_op | source)
XLA Modules:
  0.0 136.3 jit_solution(12416656887563019985)
XLA Ops:
  0.6 0.7 copy.14
  1.4 0.0 copy-start
  1.4 0.1 eq.16
  1.4 0.6 copy-done
  2.1 0.1 broadcast_in_dim.21
  2.2 0.6 select_reduce_fusion.routed_ref
  2.8 129.8 %window.1 = (bf16[4,32,1024]{2,1,0:T(8,128)(2,1)}, bf16[384,1024]{1,0:T(8,128)(2,1)}) custom-call(bf16[4,32,1024]{2,1,0:T(8,128)(2,1)} %bitcast.16, bf16[32,1024]{1,0:T(8,128)(2,1)} %bitcast.17, bf16[4,32,1024]{2,1,0:T(8,128)(2,1)} %loss_ref.1, f32[16,128]{1,0:T(8,128)} %select_reduce_fusion.routed_ref, bf16[1024,384]{1,0:T(8,128)(2,1)} %bitcast.13, ...), custom_call_target="tpu_custom_call" | custom-call | flops 9663676416 | bytes 3145728 | tf_op jit(solution)/shard_map/window/pallas_call | solution.py:293
  132.6 1.7 %copy.18 = bf16[1,4,32,1024]{3,2,1,0:T(8,128)(2,1)} copy(bf16[1,4,32,1024]{3,2,1,0:T(8,128)(2,1)} %bitcast.12) | data formatting | bytes 524288
  134.2 2.1 %copy.19 = bf16[1,1,384,1024]{3,2,1,0:T(8,128)(2,1)} copy(bf16[1,1,384,1024]{3,2,1,0:T(8,128)(2,1)} %bitcast.11) | data formatting | bytes 1572864
  (1 shorter events, 0.0 us)
Async XLA Ops:
  1.4 0.7 copy-start

commit v3 on v2

v3 whole, which is shorter than its diff:
```python
import functools

import jax
import jax.numpy as jnp
from jax import lax
from jax.experimental import pallas as pl
from jax.experimental.pallas import tpu as pltpu
from jax.sharding import PartitionSpec as P

MESH = pl.DeviceIdType.MESH
BF16 = jnp.bfloat16
F32 = jnp.float32
HALVES = 2


def kernel(
    sections, lines,
    acts_ref, carried_ref, loss_ref, routed_ref, gate_ref, up_ref, down_ref,
    out_ref, down_out_ref,
    acts_all, inc_all, routed_all, wide, wide_t, down_t, columns,
    steep, active_buf, hidden_buf, grad_buf, total,
    part, core_in, x_out, x_in, z_out, z_in, own_sum,
    ag_send, ag_recv, rs_send, rs_recv, relay_send, relay_recv,
):
    units, tokens, width = acts_ref.shape
    halves = carried_ref.shape[0]
    experts = 4 * lines
    count = experts * tokens
    ff = gate_ref.shape[1]
    section = lax.axis_index("section")
    me = lax.axis_index("expert")
    a = me // 4
    b = lax.rem(me // 2, 2)
    c = lax.rem(me, 2)
    nb, nc = 1 - b, 1 - c
    g = b * 2 + c
    ng = nb * 2 + c
    x_peer = a * 4 + nb * 2 + c
    core_peer = a * 4 + b * 2 + nc
    is_last = section == sections - 1

    def line_at(j):
        return lax.rem(a + j, lines)

    def line_peer(j):
        return line_at(j) * 4 + g

    def line_back(j):
        return lax.rem(a + lines - j, lines)

    def rows_of(kind_buf, t):
        return kind_buf if t is None else kind_buf.at[t]

    def gather_copy(buf, t, kind, index, ref_of, target):
        ref = ref_of(rows_of(buf, t))
        return pltpu.make_async_remote_copy(
            src_ref=ref, dst_ref=ref,
            send_sem=ag_send.at[kind, index], recv_sem=ag_recv.at[kind, index],
            device_id={"expert": target}, device_id_type=MESH,
        )

    def z_copy(buf, t, kind, j):
        return gather_copy(buf, t, kind, j - 1, lambda r: r.at[g, a], line_peer(j))

    def x_copy(buf, t, kind, j):
        return gather_copy(buf, t, kind, lines - 1 + j, lambda r: r.at[g, line_back(j)], x_peer)

    def core_copy(buf, t, kind, i):
        group = g if i == 0 else ng
        return gather_copy(buf, t, kind, 2 * lines - 1 + i, lambda r: r.at[group], core_peer)

    def gather_start(buf, t, kind):
        for j in range(1, lines):
            z_copy(buf, t, kind, j).start()
        x_copy(buf, t, kind, 0).start()

    def gather_lines(buf, t, kind):
        for j in range(1, lines):
            z_copy(buf, t, kind, j).wait_recv()
            x_copy(buf, t, kind, j).start()
        core_copy(buf, t, kind, 0).start()

    def gather_cross(buf, t, kind):
        for j in range(lines):
            x_copy(buf, t, kind, j).wait_recv()
        core_copy(buf, t, kind, 1).start()

    def gather_drain(buf, t, kind):
        for j in range(1, lines):
            z_copy(buf, t, kind, j).wait_send()
        for j in range(lines):
            x_copy(buf, t, kind, j).wait_send()
        for i in range(2):
            core_copy(buf, t, kind, i).wait_send()

    def acts_kind(t):
        return 1 + t

    def inc_kind(t):
        return 1 + units + t

    def back_copy(t, index, src, dst, target):
        return pltpu.make_async_remote_copy(
            src_ref=src, dst_ref=dst,
            send_sem=rs_send.at[t, index], recv_sem=rs_recv.at[t, index],
            device_id={"expert": target}, device_id_type=MESH,
        )

    def back_core(t, i):
        group = (nb if i == 0 else b) * 2 + nc
        return back_copy(t, i, part.at[t, group], core_in.at[t, i], core_peer)

    def back_x(t, j):
        return back_copy(t, 2 + j, x_out.at[t, line_at(j)], x_in.at[t, line_at(j)], x_peer)

    def back_z(t, j):
        return back_copy(t, 1 + lines + j, z_out.at[t, j - 1], z_in.at[t, j - 1], line_peer(j))

    def relay(t):
        down_one = lax.rem(section + sections - 1, sections)
        return pltpu.make_async_remote_copy(
            src_ref=out_ref.at[t], dst_ref=inc_all.at[t + halves, g, a],
            send_sem=relay_send.at[t], recv_sem=relay_recv.at[t],
            device_id={"section": down_one}, device_id_type=MESH,
        )

    barrier = pltpu.get_barrier_semaphore()
    for j in range(1, lines):
        pl.semaphore_signal(barrier, inc=1, device_id={"expert": line_peer(j)}, device_id_type=MESH)
    for peer in (x_peer, core_peer):
        pl.semaphore_signal(barrier, inc=1, device_id={"expert": peer}, device_id_type=MESH)
    for step in (1, sections - 1):
        other = lax.rem(section + step, sections)
        pl.semaphore_signal(barrier, inc=1, device_id={"section": other}, device_id_type=MESH)

    acts_all[:, g, a] = acts_ref[...]
    routed_all[g, a] = routed_ref[...]

    @pl.when(is_last)
    def _():
        inc_all[:, g, a] = loss_ref[...]

    @pl.when(jnp.logical_not(is_last))
    def _():
        inc_all[:halves, g, a] = carried_ref[...]

    pl.semaphore_wait(barrier, lines + 3)

    def forward(u):
        rows = acts_all[u].reshape(count, width)
        pre = jnp.dot(rows, wide[...], preferred_element_type=F32)
        gate_pre, up_pre = pre[:, :ff], pre[:, ff:]
        sigma = 1.0 / (1.0 + jnp.exp(-gate_pre))
        active = gate_pre * sigma
        hidden_buf[...] = (active * up_pre).astype(BF16)
        steep[...] = up_pre * sigma * (1.0 + gate_pre * (1.0 - sigma))
        active_buf[...] = active

    def backward(u):
        scale = columns[pl.ds(pl.multiple_of(u * tokens, tokens), tokens), :]
        for p in range(experts):
            block = inc_all[u, p // lines, p % lines].astype(F32)
            grad_buf[pl.ds(p * tokens, tokens), :] = (block * scale[:, p : p + 1]).astype(BF16)
        hidden_grad = jnp.dot(grad_buf[...], down_t[...], preferred_element_type=F32)
        both = jnp.concatenate(
            [(hidden_grad * steep[...]).astype(BF16), (hidden_grad * active_buf[...]).astype(BF16)], axis=1
        )
        row_grad = jnp.dot(both, wide_t[...], preferred_element_type=F32)
        part[u] = row_grad.astype(BF16).reshape(4, lines, tokens, width)

    def core_arrived(buf, u, kind):
        for i in range(2):
            core_copy(buf, u, kind, i).wait_recv()

    gather_start(routed_all, None, 0)
    gather_start(acts_all, 0, acts_kind(0))
    gather_start(inc_all, 0, inc_kind(0))
    gather_start(acts_all, 1, acts_kind(1))
    wide[:, :ff] = gate_ref[...]
    wide[:, ff:] = up_ref[...]
    wide_t[:ff, :] = gate_ref[...].T
    wide_t[ff:, :] = up_ref[...].T
    down_t[...] = down_ref[...].T
    total[...] = jnp.zeros_like(total)
    gather_lines(routed_all, None, 0)
    gather_lines(acts_all, 0, acts_kind(0))
    gather_lines(inc_all, 0, inc_kind(0))
    gather_cross(routed_all, None, 0)
    gather_cross(acts_all, 0, acts_kind(0))
    gather_lines(acts_all, 1, acts_kind(1))
    core_arrived(routed_all, None, 0)
    table = routed_all[...].reshape(experts, experts, units * tokens)
    mine = lax.broadcasted_iota(jnp.int32, table.shape, 1) == me
    columns[...] = jnp.sum(jnp.where(mine, table, 0.0), axis=1).T
    core_arrived(acts_all, 0, acts_kind(0))
    forward(0)
    gather_cross(inc_all, 0, inc_kind(0))
    core_arrived(inc_all, 0, inc_kind(0))

    def step(u, carry):
        more = u + 1 < units
        more_two = u + 2 < units
        backward(u)
        back_core(u, 0).start()
        back_core(u, 1).start()

        @pl.when(more)
        def _():
            @pl.when(jnp.logical_and(u + 1 >= halves, jnp.logical_not(is_last)))
            def _():
                relay(u + 1 - halves).wait_recv()

            gather_start(inc_all, u + 1, inc_kind(u + 1))

        back_core(u, 0).wait_recv()
        for j in range(lines):
            where = line_at(j)
            pair = part[u, ng, where].astype(F32) + core_in[u, 0, where].astype(F32)
            x_out[u, where] = pair.astype(BF16)
            back_x(u, j).start()

        @pl.when(more)
        def _():
            gather_cross(acts_all, u + 1, acts_kind(u + 1))

        @pl.when(more_two)
        def _():
            gather_start(acts_all, u + 2, acts_kind(u + 2))

        total[...] += lax.dot_general(
            hidden_buf[...], grad_buf[...], (((0,), (0,)), ((), ())), preferred_element_type=F32
        )

        @pl.when(more)
        def _():
            gather_lines(inc_all, u + 1, inc_kind(u + 1))
            core_arrived(acts_all, u + 1, acts_kind(u + 1))
            forward(u + 1)

        back_core(u, 1).wait_recv()
        for j in list(range(1, lines)) + [0]:
            back_x(u, j).wait_recv()
            where = line_at(j)
            quad = part[u, g, where].astype(F32) + core_in[u, 1, where].astype(F32)
            quad = quad + x_in[u, where].astype(F32)
            if j:
                z_out[u, j - 1] = quad.astype(BF16)
                back_z(u, j).start()
            else:
                own_sum[...] = quad + inc_all[u, g, a].astype(F32)

        @pl.when(more_two)
        def _():
            gather_lines(acts_all, u + 2, acts_kind(u + 2))

        @pl.when(more)
        def _():
            gather_cross(inc_all, u + 1, inc_kind(u + 1))

        result = own_sum[...]
        for j in range(1, lines):
            back_z(u, j).wait_recv()
            result = result + z_in[u, j - 1].astype(F32)
        out_ref[u] = result.astype(BF16)

        @pl.when(jnp.logical_and(u + halves < units, section > 0))
        def _():
            relay(u).start()

        @pl.when(more)
        def _():
            core_arrived(inc_all, u + 1, inc_kind(u + 1))

        return carry

    lax.fori_loop(0, units, step, 0)
    down_out_ref[...] = total[...].astype(BF16)
    gather_drain(routed_all, None, 0)

    def drain(u, carry):
        gather_drain(acts_all, u, acts_kind(u))
        gather_drain(inc_all, u, inc_kind(u))
        for i in range(2):
            back_core(u, i).wait_send()
        for j in range(lines):
            back_x(u, j).wait_send()
        for j in range(1, lines):
            back_z(u, j).wait_send()

        @pl.when(jnp.logical_and(u + halves < units, section > 0))
        def _():
            relay(u).wait_send()

        return carry

    lax.fori_loop(0, units, drain, 0)


def per_device(acts, carried, loss_grad, expert_ids, probs, w_gate, w_up, w_down):
    sections = lax.axis_size("section")
    experts = lax.axis_size("expert")
    lines = experts // 4
    ticks, tokens, width = acts.shape[1:]
    ff = w_gate.shape[3]
    hit = jnp.arange(experts, dtype=jnp.int32)[:, None, None] == expert_ids.reshape(1, ticks * tokens, -1)
    routed = jnp.sum(jnp.where(hit, probs.reshape(1, ticks * tokens, -1), 0.0), axis=2)
    halves = HALVES if tokens % (16 * HALVES) == 0 else 1
    units, rows = ticks * halves, tokens // halves
    kinds, hops = 1 + 2 * units, 2 * lines + 1
    count = experts * rows
    dma = pltpu.SemaphoreType.DMA
    vmem = pltpu.VMEM
    gathered = (units, 4, lines, rows, width)
    out, down = pl.pallas_call(
        functools.partial(kernel, sections, lines),
        out_shape=(
            jax.ShapeDtypeStruct((units, rows, width), BF16),
            jax.ShapeDtypeStruct((ff, width), BF16),
        ),
        in_specs=[pl.BlockSpec(memory_space=vmem)] * 7,
        out_specs=(pl.BlockSpec(memory_space=vmem),) * 2,
        scratch_shapes=[
            vmem(gathered, BF16), vmem(gathered, BF16), vmem((4, lines, experts, ticks * tokens), F32),
            vmem((width, 2 * ff), BF16), vmem((2 * ff, width), BF16), vmem((width, ff), BF16),
            vmem((ticks * tokens, experts), F32),
            vmem((count, ff), F32), vmem((count, ff), F32), vmem((count, ff), BF16),
            vmem((count, width), BF16), vmem((ff, width), F32),
            vmem(gathered, BF16), vmem((units, 2, lines, rows, width), BF16),
            vmem((units, lines, rows, width), BF16), vmem((units, lines, rows, width), BF16),
            vmem((units, lines - 1, rows, width), BF16), vmem((units, lines - 1, rows, width), BF16),
            vmem((rows, width), F32),
            dma((kinds, hops)), dma((kinds, hops)), dma((units, 1 + 2 * lines)), dma((units, 1 + 2 * lines)),
            dma((units,)), dma((units,)),
        ],
        compiler_params=pltpu.CompilerParams(
            collective_id=0, has_side_effects=True, vmem_limit_bytes=60 * 1024 * 1024
        ),
        cost_estimate=pl.CostEstimate(
            flops=12 * ticks * experts * tokens * width * ff, bytes_accessed=8 * width * ff, transcendentals=0
        ),
        name="window",
    )(
        acts.reshape(units, rows, width), carried.reshape(halves, rows, width),
        loss_grad.reshape(units, rows, width), routed, w_gate[0, 0], w_up[0, 0], w_down[0, 0],
    )
    return out.reshape(1, ticks, tokens, width), down[None, None]


def solution(mesh):
    return jax.shard_map(
        per_device,
        mesh=mesh,
        in_specs=(
            P("section", None, "expert", None),
            P("section", "expert", None),
            P(None, "expert", None),
            P("section", None, "expert", None),
            P("section", None, "expert", None),
            P("section", "expert", None, None),
            P("section", "expert", None, None),
            P("section", "expert", None, None),
        ),
        out_specs=(P("section", None, "expert", None), P("section", "expert", None, None)),
        check_vma=False,
    )
```

time: 137 us -> 129 us (0.942)
  Pallas kernels: 130 us -> 122 us
    pallas_call x1, Pallas kernels: 130 us -> 122 us  [per_device(): pl.pallas_call(functools.partial(kernel, sections, lines), out_shape=(jax...]
where the time goes in v3:
time: 129 us; the launch traced here: 128 us
  Pallas kernels  122 us (95%)
  local copies, waits for them, and re-layouts  5.26 us (4%)
    pallas_call x1, Pallas kernels, per_device(): pl.pallas_call(functools.partial(kernel, sections, lines), out_shape=(jax...  122 us
    unnamed x6, local copies, waits for them, and re-layouts  5.1 us

profile of v3, /device:TPU:0, one launch (start us, length us, event | category | flops | bytes accessed | tf_op | source)
XLA Modules:
  0.0 128.5 jit_solution(11758366747152509784)
XLA Ops:
  0.6 0.7 copy.14
  1.4 0.0 copy-start
  1.4 0.1 eq.16
  1.4 0.6 copy-done
  2.1 0.1 broadcast_in_dim.18
  2.2 0.6 select_reduce_fusion.routed_ref
  2.8 121.9 %window.1 = (bf16[8,16,1024]{2,1,0:T(8,128)(2,1)}, bf16[384,1024]{1,0:T(8,128)(2,1)}) custom-call(bf16[8,16,1024]{2,1,0:T(8,128)(2,1)} %bitcast.17, bf16[2,16,1024]{2,1,0:T(8,128)(2,1)} %bitcast.19, bf16[8,16,1024]{2,1,0:T(8,128)(2,1)} %bitcast.18, f32[16,128]{1,0:T(8,128)} %select_reduce_fusion.routed_ref, bf16[1024,384]{1,0:T(8,128)(2,1)} %bitcast.14, ...), custom_call_target="tpu_custom_call" | custom-call | flops 9663676416 | bytes 3145728 | tf_op jit(solution)/shard_map/window/pallas_call | solution.py:314
  124.7 1.7 %copy.18 = bf16[1,4,32,1024]{3,2,1,0:T(8,128)(2,1)} copy(bf16[1,4,32,1024]{3,2,1,0:T(8,128)(2,1)} %bitcast.13) | data formatting | bytes 524288
  126.4 2.1 %copy.19 = bf16[1,1,384,1024]{3,2,1,0:T(8,128)(2,1)} copy(bf16[1,1,384,1024]{3,2,1,0:T(8,128)(2,1)} %bitcast.12) | data formatting | bytes 1572864
  (1 shorter events, 0.0 us)
Async XLA Ops:
  1.4 0.7 copy-start

commit v4 on v3

v4 whole, which is shorter than its diff:
```python
import functools

import jax
import jax.numpy as jnp
from jax import lax
from jax.experimental import pallas as pl
from jax.experimental.pallas import tpu as pltpu
from jax.sharding import PartitionSpec as P

MESH = pl.DeviceIdType.MESH
BF16 = jnp.bfloat16
F32 = jnp.float32
HALVES = 2


def kernel(
    sections, lines,
    acts_ref, carried_ref, loss_ref, routed_ref, gate_ref, up_ref, down_ref,
    out_ref, down_out_ref,
    acts_all, inc_all, routed_all, gate_in, up_in, down_in, wide, wide_t, down_t, columns,
    steep, active_buf, hidden_buf, total, total_out, total_in,
    part, x_in, z_out, z_in, own_sum,
    ag_send, ag_recv, rs_send, rs_recv, relay_send, relay_recv, pair_send, pair_recv,
):
    units, tokens, width = acts_ref.shape
    halves = carried_ref.shape[0]
    blocks = 2 * lines
    count = blocks * tokens
    ff = gate_ref.shape[1]
    section = lax.axis_index("section")
    me = lax.axis_index("expert")
    a = me // 4
    b = lax.rem(me // 2, 2)
    c = lax.rem(me, 2)
    nb = 1 - b
    x_peer = a * 4 + nb * 2 + c
    core_peer = a * 4 + b * 2 + 1 - c
    is_last = section == sections - 1

    def line_at(j):
        return lax.rem(a + j, lines)

    def line_peer(j):
        return line_at(j) * 4 + b * 2 + c

    def line_back(j):
        return lax.rem(a + lines - j, lines)

    def gather_copy(buf, u, kind, index, where, target):
        ref = buf.at[b, where] if u is None else buf.at[u, b, where]
        return pltpu.make_async_remote_copy(
            src_ref=ref, dst_ref=ref,
            send_sem=ag_send.at[kind, index], recv_sem=ag_recv.at[kind, index],
            device_id={"expert": target}, device_id_type=MESH,
        )

    def z_copy(buf, u, kind, j):
        return gather_copy(buf, u, kind, j - 1, a, line_peer(j))

    def x_copy(buf, u, kind, j):
        return gather_copy(buf, u, kind, lines - 1 + j, line_back(j), x_peer)

    def gather_start(buf, u, kind):
        for j in range(1, lines):
            z_copy(buf, u, kind, j).start()
        x_copy(buf, u, kind, 0).start()

    def gather_lines(buf, u, kind):
        for j in range(1, lines):
            z_copy(buf, u, kind, j).wait_recv()
            x_copy(buf, u, kind, j).start()

    def gather_cross(buf, u, kind):
        for j in range(lines):
            x_copy(buf, u, kind, j).wait_recv()

    def gather_drain(buf, u, kind):
        for j in range(1, lines):
            z_copy(buf, u, kind, j).wait_send()
        for j in range(lines):
            x_copy(buf, u, kind, j).wait_send()

    def acts_kind(u):
        return 1 + u

    def inc_kind(u):
        return 1 + units + u

    def back_copy(u, index, src, dst, target):
        return pltpu.make_async_remote_copy(
            src_ref=src, dst_ref=dst,
            send_sem=rs_send.at[u, index], recv_sem=rs_recv.at[u, index],
            device_id={"expert": target}, device_id_type=MESH,
        )

    def back_x(u, j):
        return back_copy(u, j, part.at[u, nb, line_at(j)], x_in.at[u, line_at(j)], x_peer)

    def back_z(u, j):
        return back_copy(u, lines - 1 + j, z_out.at[u, j - 1], z_in.at[u, j - 1], line_peer(j))

    def relay(u):
        down_one = lax.rem(section + sections - 1, sections)
        return pltpu.make_async_remote_copy(
            src_ref=out_ref.at[u], dst_ref=inc_all.at[u + halves, b, a],
            send_sem=relay_send.at[u], recv_sem=relay_recv.at[u],
            device_id={"section": down_one}, device_id_type=MESH,
        )

    def pair_copy(index, src, dst):
        return pltpu.make_async_remote_copy(
            src_ref=src, dst_ref=dst, send_sem=pair_send.at[index], recv_sem=pair_recv.at[index],
            device_id={"expert": core_peer}, device_id_type=MESH,
        )

    swaps = [
        pair_copy(0, gate_ref, gate_in), pair_copy(1, up_ref, up_in),
        pair_copy(2, down_ref, down_in), pair_copy(3, total_out, total_in),
    ]

    barrier = pltpu.get_barrier_semaphore()
    for j in range(1, lines):
        pl.semaphore_signal(barrier, inc=1, device_id={"expert": line_peer(j)}, device_id_type=MESH)
    for peer in (x_peer, core_peer):
        pl.semaphore_signal(barrier, inc=1, device_id={"expert": peer}, device_id_type=MESH)
    for step in (1, sections - 1):
        other = lax.rem(section + step, sections)
        pl.semaphore_signal(barrier, inc=1, device_id={"section": other}, device_id_type=MESH)

    acts_all[:, b, a] = acts_ref[...]
    routed_all[b, a] = routed_ref[...]

    @pl.when(is_last)
    def _():
        inc_all[:, b, a] = loss_ref[...]

    @pl.when(jnp.logical_not(is_last))
    def _():
        inc_all[:halves, b, a] = carried_ref[...]

    pl.semaphore_wait(barrier, lines + 3)

    def forward(u):
        start = pl.multiple_of(u * tokens, tokens)
        scales = []
        for i in range(2):
            table = columns[i, pl.ds(start, tokens), :]
            column = jnp.concatenate([table[:, p : p + 1] for p in range(blocks)], axis=0)
            scales.append(jnp.broadcast_to(column, (count, ff)))
        scale = jnp.concatenate(scales, axis=1)
        rows = acts_all[u].reshape(count, width)
        pre = jnp.dot(rows, wide[...], preferred_element_type=F32)
        gate_pre, up_pre = pre[:, : 2 * ff], pre[:, 2 * ff :]
        sigma = 1.0 / (1.0 + jnp.exp(-gate_pre))
        active = gate_pre * sigma
        hidden_buf[...] = (active * up_pre * scale).astype(BF16)
        steep[...] = up_pre * sigma * (1.0 + gate_pre * (1.0 - sigma)) * scale
        active_buf[...] = active * scale

    def backward(u):
        rows = inc_all[u].reshape(count, width)
        hidden_grad = jnp.dot(rows, down_t[...], preferred_element_type=F32)
        both = jnp.concatenate(
            [(hidden_grad * steep[...]).astype(BF16), (hidden_grad * active_buf[...]).astype(BF16)], axis=1
        )
        row_grad = jnp.dot(both, wide_t[...], preferred_element_type=F32)
        part[u] = row_grad.astype(BF16).reshape(2, lines, tokens, width)

    gather_start(routed_all, None, 0)
    gather_start(acts_all, 0, acts_kind(0))
    for swap in swaps[:3]:
        swap.start()
    gather_start(inc_all, 0, inc_kind(0))
    gather_start(acts_all, 1, acts_kind(1))
    wide[:, :ff] = gate_ref[...]
    wide[:, 2 * ff : 3 * ff] = up_ref[...]
    gather_lines(routed_all, None, 0)
    gather_lines(acts_all, 0, acts_kind(0))
    gather_lines(inc_all, 0, inc_kind(0))
    wide_t[:ff, :] = gate_ref[...].T
    wide_t[2 * ff : 3 * ff, :] = up_ref[...].T
    down_t[:, :ff] = down_ref[...].T
    gather_lines(acts_all, 1, acts_kind(1))
    total[...] = jnp.zeros_like(total)
    gather_cross(routed_all, None, 0)
    experts = 4 * lines
    table = routed_all[...].reshape(blocks, experts, units * tokens)
    names = lax.broadcasted_iota(jnp.int32, table.shape, 1)
    columns[0] = jnp.sum(jnp.where(names == me, table, 0.0), axis=1).T
    columns[1] = jnp.sum(jnp.where(names == core_peer, table, 0.0), axis=1).T
    swaps[0].wait_recv()
    wide[:, ff : 2 * ff] = gate_in[...]
    wide_t[ff : 2 * ff, :] = gate_in[...].T
    swaps[1].wait_recv()
    wide[:, 3 * ff :] = up_in[...]
    wide_t[3 * ff :, :] = up_in[...].T
    gather_cross(acts_all, 0, acts_kind(0))
    forward(0)
    swaps[2].wait_recv()
    down_t[:, ff:] = down_in[...].T
    gather_cross(inc_all, 0, inc_kind(0))

    def step(u, carry):
        more = u + 1 < units
        more_two = u + 2 < units
        backward(u)
        for j in range(lines):
            back_x(u, j).start()

        @pl.when(more)
        def _():
            @pl.when(jnp.logical_and(u + 1 >= halves, jnp.logical_not(is_last)))
            def _():
                relay(u + 1 - halves).wait_recv()

            gather_start(inc_all, u + 1, inc_kind(u + 1))

        @pl.when(more_two)
        def _():
            gather_start(acts_all, u + 2, acts_kind(u + 2))

        total[...] += lax.dot_general(
            hidden_buf[...], inc_all[u].reshape(count, width), (((0,), (0,)), ((), ())),
            preferred_element_type=F32,
        )

        @pl.when(more)
        def _():
            gather_cross(acts_all, u + 1, acts_kind(u + 1))
            forward(u + 1)
            gather_lines(inc_all, u + 1, inc_kind(u + 1))

        for j in list(range(1, lines)) + [0]:
            back_x(u, j).wait_recv()
            where = line_at(j)
            quad = part[u, b, where].astype(F32) + x_in[u, where].astype(F32)
            if j:
                z_out[u, j - 1] = quad.astype(BF16)
                back_z(u, j).start()
            else:
                own_sum[...] = quad + inc_all[u, b, a].astype(F32)

        @pl.when(more_two)
        def _():
            gather_lines(acts_all, u + 2, acts_kind(u + 2))

        @pl.when(jnp.logical_not(more))
        def _():
            total_out[...] = total[ff:, :].astype(BF16)
            swaps[3].start()

        result = own_sum[...]
        for j in range(1, lines):
            back_z(u, j).wait_recv()
            result = result + z_in[u, j - 1].astype(F32)
        out_ref[u] = result.astype(BF16)

        @pl.when(jnp.logical_and(u + halves < units, section > 0))
        def _():
            relay(u).start()

        @pl.when(more)
        def _():
            gather_cross(inc_all, u + 1, inc_kind(u + 1))

        return carry

    lax.fori_loop(0, units, step, 0)
    swaps[3].wait_recv()
    down_out_ref[...] = (total[:ff, :] + total_in[...].astype(F32)).astype(BF16)
    gather_drain(routed_all, None, 0)
    for swap in swaps:
        swap.wait_send()

    def drain(u, carry):
        gather_drain(acts_all, u, acts_kind(u))
        gather_drain(inc_all, u, inc_kind(u))
        for j in range(lines):
            back_x(u, j).wait_send()
        for j in range(1, lines):
            back_z(u, j).wait_send()

        @pl.when(jnp.logical_and(u + halves < units, section > 0))
        def _():
            relay(u).wait_send()

        return carry

    lax.fori_loop(0, units, drain, 0)


def per_device(acts, carried, loss_grad, expert_ids, probs, w_gate, w_up, w_down):
    sections = lax.axis_size("section")
    experts = lax.axis_size("expert")
    lines = experts // 4
    ticks, tokens, width = acts.shape[1:]
    ff = w_gate.shape[3]
    hit = jnp.arange(experts, dtype=jnp.int32)[:, None, None] == expert_ids.reshape(1, ticks * tokens, -1)
    routed = jnp.sum(jnp.where(hit, probs.reshape(1, ticks * tokens, -1), 0.0), axis=2)
    halves = HALVES
    units, rows = ticks * halves, tokens // halves
    kinds, hops = 1 + 2 * units, 2 * lines - 1
    count = 2 * lines * rows
    dma = pltpu.SemaphoreType.DMA
    vmem = pltpu.VMEM
    gathered = (units, 2, lines, rows, width)
    out, down = pl.pallas_call(
        functools.partial(kernel, sections, lines),
        out_shape=(
            jax.ShapeDtypeStruct((units, rows, width), BF16),
            jax.ShapeDtypeStruct((ff, width), BF16),
        ),
        in_specs=[pl.BlockSpec(memory_space=vmem)] * 7,
        out_specs=(pl.BlockSpec(memory_space=vmem),) * 2,
        scratch_shapes=[
            vmem(gathered, BF16), vmem(gathered, BF16), vmem((2, lines, experts, ticks * tokens), F32),
            vmem((width, ff), BF16), vmem((width, ff), BF16), vmem((ff, width), BF16),
            vmem((width, 4 * ff), BF16), vmem((4 * ff, width), BF16), vmem((width, 2 * ff), BF16),
            vmem((2, ticks * tokens, 2 * lines), F32),
            vmem((count, 2 * ff), F32), vmem((count, 2 * ff), F32), vmem((count, 2 * ff), BF16),
            vmem((2 * ff, width), F32), vmem((ff, width), BF16), vmem((ff, width), BF16),
            vmem(gathered, BF16), vmem((units, lines, rows, width), BF16),
            vmem((units, lines - 1, rows, width), BF16), vmem((units, lines - 1, rows, width), BF16),
            vmem((rows, width), F32),
            dma((kinds, hops)), dma((kinds, hops)), dma((units, hops)), dma((units, hops)),
            dma((units,)), dma((units,)), dma((4,)), dma((4,)),
        ],
        compiler_params=pltpu.CompilerParams(
            collective_id=0, has_side_effects=True, vmem_limit_bytes=60 * 1024 * 1024
        ),
        cost_estimate=pl.CostEstimate(
            flops=12 * ticks * experts * tokens * width * ff, bytes_accessed=8 * width * ff, transcendentals=0
        ),
        name="window",
    )(
        acts.reshape(units, rows, width), carried.reshape(halves, rows, width),
        loss_grad.reshape(units, rows, width), routed, w_gate[0, 0], w_up[0, 0], w_down[0, 0],
    )
    return out.reshape(1, ticks, tokens, width), down[None, None]


def solution(mesh):
    return jax.shard_map(
        per_device,
        mesh=mesh,
        in_specs=(
            P("section", None, "expert", None),
            P("section", "expert", None),
            P(None, "expert", None),
            P("section", None, "expert", None),
            P("section", None, "expert", None),
            P("section", "expert", None, None),
            P("section", "expert", None, None),
            P("section", "expert", None, None),
        ),
        out_specs=(P("section", None, "expert", None), P("section", "expert", None, None)),
        check_vma=False,
    )
```

time: 129 us -> 121 us (0.938)
  Pallas kernels: 122 us -> 114 us
    pallas_call x1, Pallas kernels: 122 us -> 114 us  [per_device(): pl.pallas_call(functools.partial(kernel, sections, lines), out_shape=(jax...]
where the time goes in v4:
time: 121 us
  Pallas kernels  114 us (94%)
  local copies, waits for them, and re-layouts  5.26 us (4%)
    pallas_call x1, Pallas kernels, per_device(): pl.pallas_call(functools.partial(kernel, sections, lines), out_shape=(jax...  114 us
    unnamed x6, local copies, waits for them, and re-layouts  5.1 us

profile of v4, /device:TPU:0, one launch (start us, length us, event | category | flops | bytes accessed | tf_op | source)
XLA Modules:
  0.0 120.6 jit_solution(1043611348092736322)
XLA Ops:
  0.6 0.7 copy.14
  1.4 0.0 copy-start
  1.4 0.1 eq.16
  1.4 0.6 copy-done
  2.1 0.1 broadcast_in_dim.18
  2.2 0.6 select_reduce_fusion.routed_ref
  2.8 114.1 %window.1 = (bf16[8,16,1024]{2,1,0:T(8,128)(2,1)}, bf16[384,1024]{1,0:T(8,128)(2,1)}) custom-call(bf16[8,16,1024]{2,1,0:T(8,128)(2,1)} %bitcast.17, bf16[2,16,1024]{2,1,0:T(8,128)(2,1)} %bitcast.19, bf16[8,16,1024]{2,1,0:T(8,128)(2,1)} %bitcast.18, f32[16,128]{1,0:T(8,128)} %select_reduce_fusion.routed_ref, bf16[1024,384]{1,0:T(8,128)(2,1)} %bitcast.14, ...), custom_call_target="tpu_custom_call" | custom-call | flops 9663676416 | bytes 3145728 | tf_op jit(solution)/shard_map/window/pallas_call | solution.py:307
  116.9 1.7 %copy.18 = bf16[1,4,32,1024]{3,2,1,0:T(8,128)(2,1)} copy(bf16[1,4,32,1024]{3,2,1,0:T(8,128)(2,1)} %bitcast.13) | data formatting | bytes 524288
  118.6 2.1 %copy.19 = bf16[1,1,384,1024]{3,2,1,0:T(8,128)(2,1)} copy(bf16[1,1,384,1024]{3,2,1,0:T(8,128)(2,1)} %bitcast.12) | data formatting | bytes 1572864
  (1 shorter events, 0.0 us)
Async XLA Ops:
  1.4 0.7 copy-start

commit v5 on v4

--- a/solution.py
+++ b/solution.py
@@ -15,10 +15,11 @@
 
 def kernel(
     sections, lines,
-    acts_ref, carried_ref, loss_ref, routed_ref, gate_ref, up_ref, down_ref,
-    out_ref, down_out_ref,
+    acts_ref, carried_ref, loss_ref, ids_ref, probs_ref, gate_ref, up_ref, down_ref,
+    out_wide, total, total_in,
+    out_ref,
     acts_all, inc_all, routed_all, gate_in, up_in, down_in, wide, wide_t, down_t, columns,
-    steep, active_buf, hidden_buf, total, total_out, total_in,
+    steep, active_buf, hidden_buf, total_out,
     part, x_in, z_out, z_in, own_sum,
     ag_send, ag_recv, rs_send, rs_recv, relay_send, relay_recv, pair_send, pair_recv,
 ):
@@ -128,7 +129,14 @@
         pl.semaphore_signal(barrier, inc=1, device_id={"section": other}, device_id_type=MESH)
 
     acts_all[:, b, a] = acts_ref[...]
-    routed_all[b, a] = routed_ref[...]
+    moments = range(ids_ref.shape[0])
+    names = jnp.concatenate([ids_ref[t] for t in moments], axis=1)
+    odds = jnp.concatenate([probs_ref[t] for t in moments], axis=1)
+    expert_row = lax.broadcasted_iota(jnp.int32, (4 * lines, names.shape[1]), 0)
+    routed = jnp.zeros(expert_row.shape, F32)
+    for k in range(names.shape[0]):
+        routed = routed + jnp.where(expert_row == names[k : k + 1, :], odds[k : k + 1, :], 0.0)
+    routed_all[b, a] = routed
 
     @pl.when(is_last)
     def _():
@@ -253,6 +261,7 @@
         for j in range(1, lines):
             back_z(u, j).wait_recv()
             result = result + z_in[u, j - 1].astype(F32)
+        out_wide[u] = result
         out_ref[u] = result.astype(BF16)
 
         @pl.when(jnp.logical_and(u + halves < units, section > 0))
@@ -267,7 +276,6 @@
 
     lax.fori_loop(0, units, step, 0)
     swaps[3].wait_recv()
-    down_out_ref[...] = (total[:ff, :] + total_in[...].astype(F32)).astype(BF16)
     gather_drain(routed_all, None, 0)
     for swap in swaps:
         swap.wait_send()
@@ -295,8 +303,6 @@
     lines = experts // 4
     ticks, tokens, width = acts.shape[1:]
     ff = w_gate.shape[3]
-    hit = jnp.arange(experts, dtype=jnp.int32)[:, None, None] == expert_ids.reshape(1, ticks * tokens, -1)
-    routed = jnp.sum(jnp.where(hit, probs.reshape(1, ticks * tokens, -1), 0.0), axis=2)
     halves = HALVES
     units, rows = ticks * halves, tokens // halves
     kinds, hops = 1 + 2 * units, 2 * lines - 1
@@ -304,21 +310,23 @@
     dma = pltpu.SemaphoreType.DMA
     vmem = pltpu.VMEM
     gathered = (units, 2, lines, rows, width)
-    out, down = pl.pallas_call(
+    out, down, other_down = pl.pallas_call(
         functools.partial(kernel, sections, lines),
         out_shape=(
-            jax.ShapeDtypeStruct((units, rows, width), BF16),
+            jax.ShapeDtypeStruct((units, rows, width), F32),
+            jax.ShapeDtypeStruct((2 * ff, width), F32),
             jax.ShapeDtypeStruct((ff, width), BF16),
         ),
-        in_specs=[pl.BlockSpec(memory_space=vmem)] * 7,
-        out_specs=(pl.BlockSpec(memory_space=vmem),) * 2,
+        in_specs=[pl.BlockSpec(memory_space=vmem)] * 8,
+        out_specs=(pl.BlockSpec(memory_space=vmem),) * 3,
         scratch_shapes=[
+            vmem((units, rows, width), BF16),
             vmem(gathered, BF16), vmem(gathered, BF16), vmem((2, lines, experts, ticks * tokens), F32),
             vmem((width, ff), BF16), vmem((width, ff), BF16), vmem((ff, width), BF16),
             vmem((width, 4 * ff), BF16), vmem((4 * ff, width), BF16), vmem((width, 2 * ff), BF16),
             vmem((2, ticks * tokens, 2 * lines), F32),
             vmem((count, 2 * ff), F32), vmem((count, 2 * ff), F32), vmem((count, 2 * ff), BF16),
-            vmem((2 * ff, width), F32), vmem((ff, width), BF16), vmem((ff, width), BF16),
+            vmem((ff, width), BF16),
             vmem(gathered, BF16), vmem((units, lines, rows, width), BF16),
             vmem((units, lines - 1, rows, width), BF16), vmem((units, lines - 1, rows, width), BF16),
             vmem((rows, width), F32),
@@ -334,9 +342,11 @@
         name="window",
     )(
         acts.reshape(units, rows, width), carried.reshape(halves, rows, width),
-        loss_grad.reshape(units, rows, width), routed, w_gate[0, 0], w_up[0, 0], w_down[0, 0],
+        loss_grad.reshape(units, rows, width),
+        jnp.swapaxes(expert_ids[0], 1, 2), jnp.swapaxes(probs[0], 1, 2), w_gate[0, 0], w_up[0, 0], w_down[0, 0],
     )
-    return out.reshape(1, ticks, tokens, width), down[None, None]
+    down = down[:ff] + other_down.astype(F32)
+    return out.reshape(1, ticks, tokens, width).astype(BF16), down.astype(BF16)[None, None]
 
 
 def solution(mesh):

time: 121 us -> 121 us (level)
  local copies, waits for them, and re-layouts: 5.26 us -> 0 us
  other arithmetic: 0.62 us -> 4.57 us
    unnamed x6 -> x0, local copies, waits for them, and re-layouts: 5.1 us -> none
    broadcast_in_dim x0 -> x1, other arithmetic: none -> 2.79 us  [per_device(): down.astype(BF16)[None, None]]
    convert_element_type x0 -> x1, other arithmetic: none -> 1.78 us  [per_device(): out.reshape(1, ticks, tokens, width).astype(BF16)]
where the time goes in v5:
time: 121 us; the launch traced here: 120 us
  Pallas kernels  115 us (95%)
  other arithmetic  4.57 us (4%)
    pallas_call x1, Pallas kernels, per_device(): pl.pallas_call(functools.partial(kernel, sections, lines), out_shape=(jax...  115 us
    broadcast_in_dim x1, other arithmetic, per_device(): down.astype(BF16)[None, None]  2.79 us

profile of v5, /device:TPU:0, one launch (start us, length us, event | category | flops | bytes accessed | tf_op | source)
XLA Modules:
  0.0 120.3 jit_solution(4837200705695247420)
XLA Ops:
  0.6 115.1 %window.1 = (f32[8,16,1024]{2,1,0:T(8,128)}, f32[768,1024]{1,0:T(8,128)}, bf16[384,1024]{1,0:T(8,128)(2,1)}) custom-call(bf16[8,16,1024]{2,1,0:T(8,128)(2,1)} %bitcast.19, bf16[2,16,1024]{2,1,0:T(8,128)(2,1)} %bitcast.21, bf16[8,16,1024]{2,1,0:T(8,128)(2,1)} %bitcast.20, s32[4,8,32]{2,1,0:T(8,128)} %bitcast.22, f32[4,8,32]{2,1,0:T(8,128)} %bitcast.23, ...), custom_call_target="tpu_custom_call" | custom-call | flops 9663676416 | bytes 3145728 | tf_op jit(solution)/shard_map/window/pallas_call | solution.py:313
  115.8 1.8 %convert_element_type.20 = bf16[8,16,1024]{2,1,0:T(8,128)(2,1)} convert(f32[8,16,1024]{2,1,0:T(8,128)} %get-tuple-element.5) | non-fusion elementwise | flops 131072 | bytes 786432 | tf_op jit(solution)/shard_map/convert_element_type | solution.py:349
  117.6 2.8 %fusion = bf16[1,1,384,1024]{3,2,1,0:T(8,128)(2,1)} fusion(bf16[384,1024]{1,0:T(8,128)(2,1)} %get-tuple-element.7, f32[768,1024]{1,0:T(8,128)} %get-tuple-element.6), kind=kLoop, calls=%fused_computation.1 | loop fusion | flops 1179648 | bytes 3145728 | tf_op jit(solution)/shard_map/broadcast_in_dim | solution.py:349

commit v6 on v4

--- a/solution.py
+++ b/solution.py
@@ -15,7 +15,7 @@
 
 def kernel(
     sections, lines,
-    acts_ref, carried_ref, loss_ref, routed_ref, gate_ref, up_ref, down_ref,
+    acts_ref, carried_ref, loss_ref, ids_ref, probs_ref, gate_ref, up_ref, down_ref,
     out_ref, down_out_ref,
     acts_all, inc_all, routed_all, gate_in, up_in, down_in, wide, wide_t, down_t, columns,
     steep, active_buf, hidden_buf, total, total_out, total_in,
@@ -128,7 +128,14 @@
         pl.semaphore_signal(barrier, inc=1, device_id={"section": other}, device_id_type=MESH)
 
     acts_all[:, b, a] = acts_ref[...]
-    routed_all[b, a] = routed_ref[...]
+    moments = range(ids_ref.shape[0])
+    names = jnp.concatenate([ids_ref[t] for t in moments], axis=1)
+    odds = jnp.concatenate([probs_ref[t] for t in moments], axis=1)
+    expert_row = lax.broadcasted_iota(jnp.int32, (4 * lines, names.shape[1]), 0)
+    routed = jnp.zeros(expert_row.shape, F32)
+    for k in range(names.shape[0]):
+        routed = routed + jnp.where(expert_row == names[k : k + 1, :], odds[k : k + 1, :], 0.0)
+    routed_all[b, a] = routed
 
     @pl.when(is_last)
     def _():
@@ -295,8 +302,6 @@
     lines = experts // 4
     ticks, tokens, width = acts.shape[1:]
     ff = w_gate.shape[3]
-    hit = jnp.arange(experts, dtype=jnp.int32)[:, None, None] == expert_ids.reshape(1, ticks * tokens, -1)
-    routed = jnp.sum(jnp.where(hit, probs.reshape(1, ticks * tokens, -1), 0.0), axis=2)
     halves = HALVES
     units, rows = ticks * halves, tokens // halves
     kinds, hops = 1 + 2 * units, 2 * lines - 1
@@ -310,7 +315,7 @@
             jax.ShapeDtypeStruct((units, rows, width), BF16),
             jax.ShapeDtypeStruct((ff, width), BF16),
         ),
-        in_specs=[pl.BlockSpec(memory_space=vmem)] * 7,
+        in_specs=[pl.BlockSpec(memory_space=vmem)] * 8,
         out_specs=(pl.BlockSpec(memory_space=vmem),) * 2,
         scratch_shapes=[
             vmem(gathered, BF16), vmem(gathered, BF16), vmem((2, lines, experts, ticks * tokens), F32),
@@ -334,7 +339,8 @@
         name="window",
     )(
         acts.reshape(units, rows, width), carried.reshape(halves, rows, width),
-        loss_grad.reshape(units, rows, width), routed, w_gate[0, 0], w_up[0, 0], w_down[0, 0],
+        loss_grad.reshape(units, rows, width),
+        jnp.swapaxes(expert_ids[0], 1, 2), jnp.swapaxes(probs[0], 1, 2), w_gate[0, 0], w_up[0, 0], w_down[0, 0],
     )
     return out.reshape(1, ticks, tokens, width), down[None, None]
 

time: 121 us -> 119 us (0.983)
  local copies, waits for them, and re-layouts: 5.26 us -> 3.73 us
    unnamed x6 -> x2, local copies, waits for them, and re-layouts: 5.1 us -> 3.73 us
where the time goes in v6:
time: 119 us
  Pallas kernels  114 us (96%)
  local copies, waits for them, and re-layouts  3.73 us (3%)
    pallas_call x1, Pallas kernels, per_device(): pl.pallas_call(functools.partial(kernel, sections, lines), out_shape=(jax...  114 us
    unnamed x2, local copies, waits for them, and re-layouts  3.73 us

profile of v6, /device:TPU:0, one launch (start us, length us, event | category | flops | bytes accessed | tf_op | source)
XLA Modules:
  0.0 118.5 jit_solution(14408423833365174578)
XLA Ops:
  0.6 114.1 %window.1 = (bf16[8,16,1024]{2,1,0:T(8,128)(2,1)}, bf16[384,1024]{1,0:T(8,128)(2,1)}) custom-call(bf16[8,16,1024]{2,1,0:T(8,128)(2,1)} %bitcast.19, bf16[2,16,1024]{2,1,0:T(8,128)(2,1)} %bitcast.21, bf16[8,16,1024]{2,1,0:T(8,128)(2,1)} %bitcast.20, s32[4,8,32]{2,1,0:T(8,128)} %bitcast.22, f32[4,8,32]{2,1,0:T(8,128)} %bitcast.23, bf16[1024,384]{1,0:T(8,128)(2,1)} %bitcast.16, ...), custom_call_target="tpu_custom_call" | custom-call | flops 9663676416 | bytes 3145728 | tf_op jit(solution)/shard_map/window/pallas_call | solution.py:312
  114.8 1.7 %copy.12 = bf16[1,4,32,1024]{3,2,1,0:T(8,128)(2,1)} copy(bf16[1,4,32,1024]{3,2,1,0:T(8,128)(2,1)} %bitcast.15) | data formatting | bytes 524288
  116.4 2.1 %copy.13 = bf16[1,1,384,1024]{3,2,1,0:T(8,128)(2,1)} copy(bf16[1,1,384,1024]{3,2,1,0:T(8,128)(2,1)} %bitcast.14) | data formatting | bytes 1572864
